TPU v7x, 32 devices: a whole 2x2x4 slice. The times are simulated.
32 devices in a mesh: dir: 4 (over x, core), elem: 8 (over z, y).
Axes of the slice: x: 2, y: 2, z: 4, core: 2. Of those that a mesh axis runs over, the one named last changes fastest.
Arguments:
- panel_angles: float32 [2, 16384], P(None, 'elem'), may hold values from -3.140625 to 3.140625
- impedance: float32 [16384], P('elem'), may hold values from 0.3 to 3
- quad_count: int32 [16384], P('elem'), may hold values from 1 to 4
- receivers: int32 [1024], replicated, may hold values from 0 to 4095
- farfield_data: float32 [2, 64, 1024], P(None, 'dir'), may hold values from -24 to 24
- warm_density: float32 [2, 64, 16384], P(None, 'dir', 'elem'), may hold values from -6 to 6
Outputs:
- gradient: float32 [16384], P('elem')
- density: float32 [2, 64, 16384], P(None, 'dir', 'elem')
Inputs may be any that keep to these rules, and one draw needn't show every extreme that they name: Index into a lattice of 4096 directions; receivers may share an index.
All inputs are finite; a program needn't handle non-finite values.
Results may differ from a plain program's by a relative error of at most 0.0038.
Values may be sent and summed in bfloat16 or wider, within the bound.
A program may use at most 256 MiB of HBM per device.

v0:
```python
from functools import partial
import math

import jax
import jax.numpy as jnp
from jax import lax
from jax.sharding import PartitionSpec as P

PANELS = 16384
ITERS = 1
RBANK = 4096


WAVENUM = 32.0
SOFTEN = 0.0025
tile_rows = 512


def positions(angles):
    phi = angles[0]
    psi = angles[1]
    return jnp.stack(
        [4.0 * jnp.cos(psi), jnp.sin(psi) * jnp.cos(phi), 0.6 * jnp.sin(psi) * jnp.sin(phi)]
    )


def weights(counts):
    return counts.astype(jnp.float32) * (0.5 / (4.0 * math.sqrt(PANELS)))


def lattice(index, count):
    where = index.astype(jnp.float32)
    height = 1.0 - (2.0 * where + 1.0) / count
    radius = jnp.sqrt(1.0 - height * height)
    turn = where * (math.pi * (3.0 - math.sqrt(5.0)))
    return jnp.stack([radius * jnp.cos(turn), radius * jnp.sin(turn), height])


def plane(dvec, pos):
    phase = WAVENUM * jnp.sum(dvec[:, :, None] * pos[:, None, :], axis=0)
    return jnp.stack([jnp.cos(phase), jnp.sin(phase)])


def far_table(pos, rdir):
    theta = WAVENUM * jnp.sum(pos[:, :, None] * rdir[:, None, :], axis=0)
    return (jnp.cos(theta).astype(jnp.bfloat16), jnp.sin(theta).astype(jnp.bfloat16))


def kernel_tile(src, tgt):
    dist = jnp.sum((src[:, :, None] - tgt[:, None, :]) ** 2, axis=0)
    rho = jnp.sqrt(dist + SOFTEN)
    return (
        (jnp.cos(WAVENUM * rho) / rho).astype(jnp.bfloat16),
        (jnp.sin(WAVENUM * rho) / rho).astype(jnp.bfloat16),
    )


def apply(vec, cos_t, sin_t, sign, axis):
    half = vec.shape[1]
    stacked = vec.reshape(2 * half, vec.shape[2])
    dims = (((1,), (axis,)), ((), ()))
    first = lax.dot_general(stacked, cos_t, dims, preferred_element_type=jnp.float32)
    second = lax.dot_general(stacked, sin_t, dims, preferred_element_type=jnp.float32)
    real = first[:half] - sign * second[half:]
    imag = first[half:] + sign * second[:half]
    return jnp.stack([real, imag])


def build_kernel(pos_all, pos_loc):
    total_panels = pos_all.shape[1]
    count = total_panels // tile_rows
    sources = jnp.transpose(pos_all.reshape(3, count, tile_rows), (1, 0, 2))
    cos_k, sin_k = lax.map(lambda src: kernel_tile(src, pos_loc), sources)
    rows = pos_loc.shape[1]
    return (cos_k.reshape(total_panels, rows), sin_k.reshape(total_panels, rows))


def kernel_sum(total, piece_at, cos_k, sin_k, count, sign):

    def add_block(step, acc):
        begin = step * tile_rows
        cos_t = lax.dynamic_slice_in_dim(cos_k, begin, tile_rows, 0)
        sin_t = lax.dynamic_slice_in_dim(sin_k, begin, tile_rows, 0)
        return acc + apply(piece_at(begin, tile_rows), cos_t, sin_t, sign, 0)

    return lax.fori_loop(0, count // tile_rows, add_block, total)


def slice_panels(piece, begin, block):
    return lax.dynamic_slice_in_dim(piece, begin, block, 2)


def on_device(panel_angles, impedance, quad_count, receivers, farfield_data, warm_density):
    rows = impedance.shape[0]
    count_dir = farfield_data.shape[1]
    ndir = count_dir * lax.axis_size("dir")
    w_loc = weights(quad_count)
    wz_loc = w_loc * impedance
    geom = jnp.concatenate([panel_angles, w_loc[None], impedance[None]], axis=0)
    whole = lax.all_gather(geom, "elem", axis=1, tiled=True)
    pos_all = positions(whole[:2])
    pos_loc = positions(panel_angles)
    cos_k, sin_k = build_kernel(pos_all, pos_loc)
    dvec = lattice(lax.axis_index("dir") * count_dir + jnp.arange(count_dir, dtype=jnp.int32), ndir)
    incident = plane(dvec, pos_loc)
    empty = jnp.zeros((2, count_dir, rows), jnp.float32)

    def spread(vec, sign):
        piece = lax.all_gather(vec, "elem", axis=2, tiled=True)
        width = piece.shape[2]
        return kernel_sum(empty, partial(slice_panels, piece), cos_k, sin_k, width, sign)

    sigmas = [warm_density]
    state = warm_density
    step = 0
    image = spread((wz_loc * state).astype(jnp.bfloat16), 1.0)
    state = incident - image
    sigmas.append(state)
    rdir = lattice(receivers, RBANK)
    cos_t, sin_t = far_table(pos_loc, rdir)
    partial_far = apply((w_loc * state).astype(jnp.bfloat16), cos_t, sin_t, -1.0, 0)
    farfield = lax.psum(partial_far, "elem")
    misfit = (farfield - farfield_data).astype(jnp.bfloat16)
    grad_local = jnp.zeros((rows,), jnp.float32)
    adjoint = None
    for step in reversed(range(ITERS)):
        adjoint = w_loc * apply(misfit, cos_t, sin_t, 1.0, 1)
        back = -spread(adjoint.astype(jnp.bfloat16), -1.0)
        grad_local = jnp.sum(back * sigmas[step], axis=(0, 1))
        adjoint = wz_loc * back
    return (lax.psum(grad_local, "dir") / ndir, state)


def solution(mesh):
    placed = (
        P(None, "elem"),
        P("elem"),
        P("elem"),
        P(),
        P(None, "dir", None),
        P(None, "dir", "elem"),
    )
    return jax.shard_map(
        on_device,
        mesh=mesh,
        in_specs=placed,
        out_specs=(P("elem"), P(None, "dir", "elem")),
        check_vma=False,
    )
```

profile of v0, /device:TPU:0, one launch (start us, length us, event | category | flops | bytes accessed | tf_op | source)
XLA Modules:
  0.0 1221.1 jit_solution(6312788987671277223)
XLA Ops:
  11.7 32.7 %all_gather.10 = f32[4,16384]{1,0:T(4,128)S(1)} all-gather(f32[4,2048]{1,0:T(4,128)S(1)} %pad_maximum_fusion.2), channel_id=1, replica_groups=mesh['dir'=4,'elem'=8] {'elem'}, dimensions={1}, use_global_device_ids=true | all-gather | bytes 294912 | tf_op jit(solution)/shard_map/all_gather | solution.py:100
  44.4 3.8 cosine_multiply_fusion.1
  48.4 597.5 %while.40 = (s32[]{:T(128)}, bf16[32,512,2048]{2,1,0:T(8,128)(2,1)}, bf16[32,512,2048]{2,1,0:T(8,128)(2,1)}, f32[32,3,512]{2,1,0:T(4,128)S(1)}, f32[3,2048]{1,0:T(4,128)S(1)}, /*index=5*/s32[]{:T(128)}) while((s32[]{:T(128)}, bf16[32,512,2048]{2,1,0:T(8,128)(2,1)}, bf16[32,512,2048]{2,1,0:T(8,128)(2,1)}, f32[32,3,512]{2,1,0:T(4,128)S(1)}, ...), condition=%wide.region_2.3_spmd, body=%wide.region_0.2_spmd.sunk | while | flops 14680066 | bytes 12626505 | solution.py:73
  49.7 17.4 %fusion.61 = (bf16[32,512,2048]{2,1,0:T(8,128)(2,1)}, bf16[32,512,2048]{2,1,0:T(8,128)(2,1)}) fusion(bf16[32,512,2048]{2,1,0:T(8,128)(2,1)} %get-tuple-element.428, s32[]{:T(128)} %get-tuple-element.426, f32[512,2048]{1,0:T(8,128)S(1)} %multiply_reduce_fusion.5, bf16[32,512,2048]{2,1,0:T(8,128)(2,1)} %get-tuple-element.427), kind=kLoop, calls=%fused_computation.7.clone.1 | loop fusion | flops 6291456 | bytes 8389120 | tf_op jit(solution)/shard_map/while/body/jit(dynamic_update_index_in_dim)/dynamic_update_slice | solution.py:73
  68.4 17.4 %fusion.61 = (bf16[32,512,2048]{2,1,0:T(8,128)(2,1)}, bf16[32,512,2048]{2,1,0:T(8,128)(2,1)}) fusion(bf16[32,512,2048]{2,1,0:T(8,128)(2,1)} %get-tuple-element.428, s32[]{:T(128)} %get-tuple-element.426, f32[512,2048]{1,0:T(8,128)S(1)} %multiply_reduce_fusion.5, bf16[32,512,2048]{2,1,0:T(8,128)(2,1)} %get-tuple-element.427), kind=kLoop, calls=%fused_computation.7.clone.1 | loop fusion | flops 6291456 | bytes 8389120 | tf_op jit(solution)/shard_map/while/body/jit(dynamic_update_index_in_dim)/dynamic_update_slice | solution.py:73
  87.1 17.4 %fusion.61 = (bf16[32,512,2048]{2,1,0:T(8,128)(2,1)}, bf16[32,512,2048]{2,1,0:T(8,128)(2,1)}) fusion(bf16[32,512,2048]{2,1,0:T(8,128)(2,1)} %get-tuple-element.428, s32[]{:T(128)} %get-tuple-element.426, f32[512,2048]{1,0:T(8,128)S(1)} %multiply_reduce_fusion.5, bf16[32,512,2048]{2,1,0:T(8,128)(2,1)} %get-tuple-element.427), kind=kLoop, calls=%fused_computation.7.clone.1 | loop fusion | flops 6291456 | bytes 8389120 | tf_op jit(solution)/shard_map/while/body/jit(dynamic_update_index_in_dim)/dynamic_update_slice | solution.py:73
  105.7 17.4 %fusion.61 = (bf16[32,512,2048]{2,1,0:T(8,128)(2,1)}, bf16[32,512,2048]{2,1,0:T(8,128)(2,1)}) fusion(bf16[32,512,2048]{2,1,0:T(8,128)(2,1)} %get-tuple-element.428, s32[]{:T(128)} %get-tuple-element.426, f32[512,2048]{1,0:T(8,128)S(1)} %multiply_reduce_fusion.5, bf16[32,512,2048]{2,1,0:T(8,128)(2,1)} %get-tuple-element.427), kind=kLoop, calls=%fused_computation.7.clone.1 | loop fusion | flops 6291456 | bytes 8389120 | tf_op jit(solution)/shard_map/while/body/jit(dynamic_update_index_in_dim)/dynamic_update_slice | solution.py:73
  124.4 17.4 %fusion.61 = (bf16[32,512,2048]{2,1,0:T(8,128)(2,1)}, bf16[32,512,2048]{2,1,0:T(8,128)(2,1)}) fusion(bf16[32,512,2048]{2,1,0:T(8,128)(2,1)} %get-tuple-element.428, s32[]{:T(128)} %get-tuple-element.426, f32[512,2048]{1,0:T(8,128)S(1)} %multiply_reduce_fusion.5, bf16[32,512,2048]{2,1,0:T(8,128)(2,1)} %get-tuple-element.427), kind=kLoop, calls=%fused_computation.7.clone.1 | loop fusion | flops 6291456 | bytes 8389120 | tf_op jit(solution)/shard_map/while/body/jit(dynamic_update_index_in_dim)/dynamic_update_slice | solution.py:73
  143.1 17.4 %fusion.61 = (bf16[32,512,2048]{2,1,0:T(8,128)(2,1)}, bf16[32,512,2048]{2,1,0:T(8,128)(2,1)}) fusion(bf16[32,512,2048]{2,1,0:T(8,128)(2,1)} %get-tuple-element.428, s32[]{:T(128)} %get-tuple-element.426, f32[512,2048]{1,0:T(8,128)S(1)} %multiply_reduce_fusion.5, bf16[32,512,2048]{2,1,0:T(8,128)(2,1)} %get-tuple-element.427), kind=kLoop, calls=%fused_computation.7.clone.1 | loop fusion | flops 6291456 | bytes 8389120 | tf_op jit(solution)/shard_map/while/body/jit(dynamic_update_index_in_dim)/dynamic_update_slice | solution.py:73
  161.8 17.4 %fusion.61 = (bf16[32,512,2048]{2,1,0:T(8,128)(2,1)}, bf16[32,512,2048]{2,1,0:T(8,128)(2,1)}) fusion(bf16[32,512,2048]{2,1,0:T(8,128)(2,1)} %get-tuple-element.428, s32[]{:T(128)} %get-tuple-element.426, f32[512,2048]{1,0:T(8,128)S(1)} %multiply_reduce_fusion.5, bf16[32,512,2048]{2,1,0:T(8,128)(2,1)} %get-tuple-element.427), kind=kLoop, calls=%fused_computation.7.clone.1 | loop fusion | flops 6291456 | bytes 8389120 | tf_op jit(solution)/shard_map/while/body/jit(dynamic_update_index_in_dim)/dynamic_update_slice | solution.py:73
  180.4 17.4 %fusion.61 = (bf16[32,512,2048]{2,1,0:T(8,128)(2,1)}, bf16[32,512,2048]{2,1,0:T(8,128)(2,1)}) fusion(bf16[32,512,2048]{2,1,0:T(8,128)(2,1)} %get-tuple-element.428, s32[]{:T(128)} %get-tuple-element.426, f32[512,2048]{1,0:T(8,128)S(1)} %multiply_reduce_fusion.5, bf16[32,512,2048]{2,1,0:T(8,128)(2,1)} %get-tuple-element.427), kind=kLoop, calls=%fused_computation.7.clone.1 | loop fusion | flops 6291456 | bytes 8389120 | tf_op jit(solution)/shard_map/while/body/jit(dynamic_update_index_in_dim)/dynamic_update_slice | solution.py:73
  199.1 17.4 %fusion.61 = (bf16[32,512,2048]{2,1,0:T(8,128)(2,1)}, bf16[32,512,2048]{2,1,0:T(8,128)(2,1)}) fusion(bf16[32,512,2048]{2,1,0:T(8,128)(2,1)} %get-tuple-element.428, s32[]{:T(128)} %get-tuple-element.426, f32[512,2048]{1,0:T(8,128)S(1)} %multiply_reduce_fusion.5, bf16[32,512,2048]{2,1,0:T(8,128)(2,1)} %get-tuple-element.427), kind=kLoop, calls=%fused_computation.7.clone.1 | loop fusion | flops 6291456 | bytes 8389120 | tf_op jit(solution)/shard_map/while/body/jit(dynamic_update_index_in_dim)/dynamic_update_slice | solution.py:73
  217.8 17.4 %fusion.61 = (bf16[32,512,2048]{2,1,0:T(8,128)(2,1)}, bf16[32,512,2048]{2,1,0:T(8,128)(2,1)}) fusion(bf16[32,512,2048]{2,1,0:T(8,128)(2,1)} %get-tuple-element.428, s32[]{:T(128)} %get-tuple-element.426, f32[512,2048]{1,0:T(8,128)S(1)} %multiply_reduce_fusion.5, bf16[32,512,2048]{2,1,0:T(8,128)(2,1)} %get-tuple-element.427), kind=kLoop, calls=%fused_computation.7.clone.1 | loop fusion | flops 6291456 | bytes 8389120 | tf_op jit(solution)/shard_map/while/body/jit(dynamic_update_index_in_dim)/dynamic_update_slice | solution.py:73
  236.4 17.4 %fusion.61 = (bf16[32,512,2048]{2,1,0:T(8,128)(2,1)}, bf16[32,512,2048]{2,1,0:T(8,128)(2,1)}) fusion(bf16[32,512,2048]{2,1,0:T(8,128)(2,1)} %get-tuple-element.428, s32[]{:T(128)} %get-tuple-element.426, f32[512,2048]{1,0:T(8,128)S(1)} %multiply_reduce_fusion.5, bf16[32,512,2048]{2,1,0:T(8,128)(2,1)} %get-tuple-element.427), kind=kLoop, calls=%fused_computation.7.clone.1 | loop fusion | flops 6291456 | bytes 8389120 | tf_op jit(solution)/shard_map/while/body/jit(dynamic_update_index_in_dim)/dynamic_update_slice | solution.py:73
  255.1 17.4 %fusion.61 = (bf16[32,512,2048]{2,1,0:T(8,128)(2,1)}, bf16[32,512,2048]{2,1,0:T(8,128)(2,1)}) fusion(bf16[32,512,2048]{2,1,0:T(8,128)(2,1)} %get-tuple-element.428, s32[]{:T(128)} %get-tuple-element.426, f32[512,2048]{1,0:T(8,128)S(1)} %multiply_reduce_fusion.5, bf16[32,512,2048]{2,1,0:T(8,128)(2,1)} %get-tuple-element.427), kind=kLoop, calls=%fused_computation.7.clone.1 | loop fusion | flops 6291456 | bytes 8389120 | tf_op jit(solution)/shard_map/while/body/jit(dynamic_update_index_in_dim)/dynamic_update_slice | solution.py:73
  273.8 17.4 %fusion.61 = (bf16[32,512,2048]{2,1,0:T(8,128)(2,1)}, bf16[32,512,2048]{2,1,0:T(8,128)(2,1)}) fusion(bf16[32,512,2048]{2,1,0:T(8,128)(2,1)} %get-tuple-element.428, s32[]{:T(128)} %get-tuple-element.426, f32[512,2048]{1,0:T(8,128)S(1)} %multiply_reduce_fusion.5, bf16[32,512,2048]{2,1,0:T(8,128)(2,1)} %get-tuple-element.427), kind=kLoop, calls=%fused_computation.7.clone.1 | loop fusion | flops 6291456 | bytes 8389120 | tf_op jit(solution)/shard_map/while/body/jit(dynamic_update_index_in_dim)/dynamic_update_slice | solution.py:73
  292.5 17.4 %fusion.61 = (bf16[32,512,2048]{2,1,0:T(8,128)(2,1)}, bf16[32,512,2048]{2,1,0:T(8,128)(2,1)}) fusion(bf16[32,512,2048]{2,1,0:T(8,128)(2,1)} %get-tuple-element.428, s32[]{:T(128)} %get-tuple-element.426, f32[512,2048]{1,0:T(8,128)S(1)} %multiply_reduce_fusion.5, bf16[32,512,2048]{2,1,0:T(8,128)(2,1)} %get-tuple-element.427), kind=kLoop, calls=%fused_computation.7.clone.1 | loop fusion | flops 6291456 | bytes 8389120 | tf_op jit(solution)/shard_map/while/body/jit(dynamic_update_index_in_dim)/dynamic_update_slice | solution.py:73
  311.1 17.4 %fusion.61 = (bf16[32,512,2048]{2,1,0:T(8,128)(2,1)}, bf16[32,512,2048]{2,1,0:T(8,128)(2,1)}) fusion(bf16[32,512,2048]{2,1,0:T(8,128)(2,1)} %get-tuple-element.428, s32[]{:T(128)} %get-tuple-element.426, f32[512,2048]{1,0:T(8,128)S(1)} %multiply_reduce_fusion.5, bf16[32,512,2048]{2,1,0:T(8,128)(2,1)} %get-tuple-element.427), kind=kLoop, calls=%fused_computation.7.clone.1 | loop fusion | flops 6291456 | bytes 8389120 | tf_op jit(solution)/shard_map/while/body/jit(dynamic_update_index_in_dim)/dynamic_update_slice | solution.py:73
  329.8 17.4 %fusion.61 = (bf16[32,512,2048]{2,1,0:T(8,128)(2,1)}, bf16[32,512,2048]{2,1,0:T(8,128)(2,1)}) fusion(bf16[32,512,2048]{2,1,0:T(8,128)(2,1)} %get-tuple-element.428, s32[]{:T(128)} %get-tuple-element.426, f32[512,2048]{1,0:T(8,128)S(1)} %multiply_reduce_fusion.5, bf16[32,512,2048]{2,1,0:T(8,128)(2,1)} %get-tuple-element.427), kind=kLoop, calls=%fused_computation.7.clone.1 | loop fusion | flops 6291456 | bytes 8389120 | tf_op jit(solution)/shard_map/while/body/jit(dynamic_update_index_in_dim)/dynamic_update_slice | solution.py:73
  348.5 17.4 %fusion.61 = (bf16[32,512,2048]{2,1,0:T(8,128)(2,1)}, bf16[32,512,2048]{2,1,0:T(8,128)(2,1)}) fusion(bf16[32,512,2048]{2,1,0:T(8,128)(2,1)} %get-tuple-element.428, s32[]{:T(128)} %get-tuple-element.426, f32[512,2048]{1,0:T(8,128)S(1)} %multiply_reduce_fusion.5, bf16[32,512,2048]{2,1,0:T(8,128)(2,1)} %get-tuple-element.427), kind=kLoop, calls=%fused_computation.7.clone.1 | loop fusion | flops 6291456 | bytes 8389120 | tf_op jit(solution)/shard_map/while/body/jit(dynamic_update_index_in_dim)/dynamic_update_slice | solution.py:73
  367.1 17.4 %fusion.61 = (bf16[32,512,2048]{2,1,0:T(8,128)(2,1)}, bf16[32,512,2048]{2,1,0:T(8,128)(2,1)}) fusion(bf16[32,512,2048]{2,1,0:T(8,128)(2,1)} %get-tuple-element.428, s32[]{:T(128)} %get-tuple-element.426, f32[512,2048]{1,0:T(8,128)S(1)} %multiply_reduce_fusion.5, bf16[32,512,2048]{2,1,0:T(8,128)(2,1)} %get-tuple-element.427), kind=kLoop, calls=%fused_computation.7.clone.1 | loop fusion | flops 6291456 | bytes 8389120 | tf_op jit(solution)/shard_map/while/body/jit(dynamic_update_index_in_dim)/dynamic_update_slice | solution.py:73
  385.8 17.4 %fusion.61 = (bf16[32,512,2048]{2,1,0:T(8,128)(2,1)}, bf16[32,512,2048]{2,1,0:T(8,128)(2,1)}) fusion(bf16[32,512,2048]{2,1,0:T(8,128)(2,1)} %get-tuple-element.428, s32[]{:T(128)} %get-tuple-element.426, f32[512,2048]{1,0:T(8,128)S(1)} %multiply_reduce_fusion.5, bf16[32,512,2048]{2,1,0:T(8,128)(2,1)} %get-tuple-element.427), kind=kLoop, calls=%fused_computation.7.clone.1 | loop fusion | flops 6291456 | bytes 8389120 | tf_op jit(solution)/shard_map/while/body/jit(dynamic_update_index_in_dim)/dynamic_update_slice | solution.py:73
  404.5 17.4 %fusion.61 = (bf16[32,512,2048]{2,1,0:T(8,128)(2,1)}, bf16[32,512,2048]{2,1,0:T(8,128)(2,1)}) fusion(bf16[32,512,2048]{2,1,0:T(8,128)(2,1)} %get-tuple-element.428, s32[]{:T(128)} %get-tuple-element.426, f32[512,2048]{1,0:T(8,128)S(1)} %multiply_reduce_fusion.5, bf16[32,512,2048]{2,1,0:T(8,128)(2,1)} %get-tuple-element.427), kind=kLoop, calls=%fused_computation.7.clone.1 | loop fusion | flops 6291456 | bytes 8389120 | tf_op jit(solution)/shard_map/while/body/jit(dynamic_update_index_in_dim)/dynamic_update_slice | solution.py:73
  423.2 17.4 %fusion.61 = (bf16[32,512,2048]{2,1,0:T(8,128)(2,1)}, bf16[32,512,2048]{2,1,0:T(8,128)(2,1)}) fusion(bf16[32,512,2048]{2,1,0:T(8,128)(2,1)} %get-tuple-element.428, s32[]{:T(128)} %get-tuple-element.426, f32[512,2048]{1,0:T(8,128)S(1)} %multiply_reduce_fusion.5, bf16[32,512,2048]{2,1,0:T(8,128)(2,1)} %get-tuple-element.427), kind=kLoop, calls=%fused_computation.7.clone.1 | loop fusion | flops 6291456 | bytes 8389120 | tf_op jit(solution)/shard_map/while/body/jit(dynamic_update_index_in_dim)/dynamic_update_slice | solution.py:73
  441.8 17.4 %fusion.61 = (bf16[32,512,2048]{2,1,0:T(8,128)(2,1)}, bf16[32,512,2048]{2,1,0:T(8,128)(2,1)}) fusion(bf16[32,512,2048]{2,1,0:T(8,128)(2,1)} %get-tuple-element.428, s32[]{:T(128)} %get-tuple-element.426, f32[512,2048]{1,0:T(8,128)S(1)} %multiply_reduce_fusion.5, bf16[32,512,2048]{2,1,0:T(8,128)(2,1)} %get-tuple-element.427), kind=kLoop, calls=%fused_computation.7.clone.1 | loop fusion | flops 6291456 | bytes 8389120 | tf_op jit(solution)/shard_map/while/body/jit(dynamic_update_index_in_dim)/dynamic_update_slice | solution.py:73
  460.5 17.4 %fusion.61 = (bf16[32,512,2048]{2,1,0:T(8,128)(2,1)}, bf16[32,512,2048]{2,1,0:T(8,128)(2,1)}) fusion(bf16[32,512,2048]{2,1,0:T(8,128)(2,1)} %get-tuple-element.428, s32[]{:T(128)} %get-tuple-element.426, f32[512,2048]{1,0:T(8,128)S(1)} %multiply_reduce_fusion.5, bf16[32,512,2048]{2,1,0:T(8,128)(2,1)} %get-tuple-element.427), kind=kLoop, calls=%fused_computation.7.clone.1 | loop fusion | flops 6291456 | bytes 8389120 | tf_op jit(solution)/shard_map/while/body/jit(dynamic_update_index_in_dim)/dynamic_update_slice | solution.py:73
  479.2 17.4 %fusion.61 = (bf16[32,512,2048]{2,1,0:T(8,128)(2,1)}, bf16[32,512,2048]{2,1,0:T(8,128)(2,1)}) fusion(bf16[32,512,2048]{2,1,0:T(8,128)(2,1)} %get-tuple-element.428, s32[]{:T(128)} %get-tuple-element.426, f32[512,2048]{1,0:T(8,128)S(1)} %multiply_reduce_fusion.5, bf16[32,512,2048]{2,1,0:T(8,128)(2,1)} %get-tuple-element.427), kind=kLoop, calls=%fused_computation.7.clone.1 | loop fusion | flops 6291456 | bytes 8389120 | tf_op jit(solution)/shard_map/while/body/jit(dynamic_update_index_in_dim)/dynamic_update_slice | solution.py:73
  497.9 17.4 %fusion.61 = (bf16[32,512,2048]{2,1,0:T(8,128)(2,1)}, bf16[32,512,2048]{2,1,0:T(8,128)(2,1)}) fusion(bf16[32,512,2048]{2,1,0:T(8,128)(2,1)} %get-tuple-element.428, s32[]{:T(128)} %get-tuple-element.426, f32[512,2048]{1,0:T(8,128)S(1)} %multiply_reduce_fusion.5, bf16[32,512,2048]{2,1,0:T(8,128)(2,1)} %get-tuple-element.427), kind=kLoop, calls=%fused_computation.7.clone.1 | loop fusion | flops 6291456 | bytes 8389120 | tf_op jit(solution)/shard_map/while/body/jit(dynamic_update_index_in_dim)/dynamic_update_slice | solution.py:73
  516.5 17.4 %fusion.61 = (bf16[32,512,2048]{2,1,0:T(8,128)(2,1)}, bf16[32,512,2048]{2,1,0:T(8,128)(2,1)}) fusion(bf16[32,512,2048]{2,1,0:T(8,128)(2,1)} %get-tuple-element.428, s32[]{:T(128)} %get-tuple-element.426, f32[512,2048]{1,0:T(8,128)S(1)} %multiply_reduce_fusion.5, bf16[32,512,2048]{2,1,0:T(8,128)(2,1)} %get-tuple-element.427), kind=kLoop, calls=%fused_computation.7.clone.1 | loop fusion | flops 6291456 | bytes 8389120 | tf_op jit(solution)/shard_map/while/body/jit(dynamic_update_index_in_dim)/dynamic_update_slice | solution.py:73
  535.2 17.4 %fusion.61 = (bf16[32,512,2048]{2,1,0:T(8,128)(2,1)}, bf16[32,512,2048]{2,1,0:T(8,128)(2,1)}) fusion(bf16[32,512,2048]{2,1,0:T(8,128)(2,1)} %get-tuple-element.428, s32[]{:T(128)} %get-tuple-element.426, f32[512,2048]{1,0:T(8,128)S(1)} %multiply_reduce_fusion.5, bf16[32,512,2048]{2,1,0:T(8,128)(2,1)} %get-tuple-element.427), kind=kLoop, calls=%fused_computation.7.clone.1 | loop fusion | flops 6291456 | bytes 8389120 | tf_op jit(solution)/shard_map/while/body/jit(dynamic_update_index_in_dim)/dynamic_update_slice | solution.py:73
  553.9 17.4 %fusion.61 = (bf16[32,512,2048]{2,1,0:T(8,128)(2,1)}, bf16[32,512,2048]{2,1,0:T(8,128)(2,1)}) fusion(bf16[32,512,2048]{2,1,0:T(8,128)(2,1)} %get-tuple-element.428, s32[]{:T(128)} %get-tuple-element.426, f32[512,2048]{1,0:T(8,128)S(1)} %multiply_reduce_fusion.5, bf16[32,512,2048]{2,1,0:T(8,128)(2,1)} %get-tuple-element.427), kind=kLoop, calls=%fused_computation.7.clone.1 | loop fusion | flops 6291456 | bytes 8389120 | tf_op jit(solution)/shard_map/while/body/jit(dynamic_update_index_in_dim)/dynamic_update_slice | solution.py:73
  572.5 17.4 %fusion.61 = (bf16[32,512,2048]{2,1,0:T(8,128)(2,1)}, bf16[32,512,2048]{2,1,0:T(8,128)(2,1)}) fusion(bf16[32,512,2048]{2,1,0:T(8,128)(2,1)} %get-tuple-element.428, s32[]{:T(128)} %get-tuple-element.426, f32[512,2048]{1,0:T(8,128)S(1)} %multiply_reduce_fusion.5, bf16[32,512,2048]{2,1,0:T(8,128)(2,1)} %get-tuple-element.427), kind=kLoop, calls=%fused_computation.7.clone.1 | loop fusion | flops 6291456 | bytes 8389120 | tf_op jit(solution)/shard_map/while/body/jit(dynamic_update_index_in_dim)/dynamic_update_slice | solution.py:73
  591.2 17.4 %fusion.61 = (bf16[32,512,2048]{2,1,0:T(8,128)(2,1)}, bf16[32,512,2048]{2,1,0:T(8,128)(2,1)}) fusion(bf16[32,512,2048]{2,1,0:T(8,128)(2,1)} %get-tuple-element.428, s32[]{:T(128)} %get-tuple-element.426, f32[512,2048]{1,0:T(8,128)S(1)} %multiply_reduce_fusion.5, bf16[32,512,2048]{2,1,0:T(8,128)(2,1)} %get-tuple-element.427), kind=kLoop, calls=%fused_computation.7.clone.1 | loop fusion | flops 6291456 | bytes 8389120 | tf_op jit(solution)/shard_map/while/body/jit(dynamic_update_index_in_dim)/dynamic_update_slice | solution.py:73
  609.9 17.4 %fusion.61 = (bf16[32,512,2048]{2,1,0:T(8,128)(2,1)}, bf16[32,512,2048]{2,1,0:T(8,128)(2,1)}) fusion(bf16[32,512,2048]{2,1,0:T(8,128)(2,1)} %get-tuple-element.428, s32[]{:T(128)} %get-tuple-element.426, f32[512,2048]{1,0:T(8,128)S(1)} %multiply_reduce_fusion.5, bf16[32,512,2048]{2,1,0:T(8,128)(2,1)} %get-tuple-element.427), kind=kLoop, calls=%fused_computation.7.clone.1 | loop fusion | flops 6291456 | bytes 8389120 | tf_op jit(solution)/shard_map/while/body/jit(dynamic_update_index_in_dim)/dynamic_update_slice | solution.py:73
  628.5 17.4 %fusion.61 = (bf16[32,512,2048]{2,1,0:T(8,128)(2,1)}, bf16[32,512,2048]{2,1,0:T(8,128)(2,1)}) fusion(bf16[32,512,2048]{2,1,0:T(8,128)(2,1)} %get-tuple-element.428, s32[]{:T(128)} %get-tuple-element.426, f32[512,2048]{1,0:T(8,128)S(1)} %multiply_reduce_fusion.5, bf16[32,512,2048]{2,1,0:T(8,128)(2,1)} %get-tuple-element.427), kind=kLoop, calls=%fused_computation.7.clone.1 | loop fusion | flops 6291456 | bytes 8389120 | tf_op jit(solution)/shard_map/while/body/jit(dynamic_update_index_in_dim)/dynamic_update_slice | solution.py:73
  646.2 4.8 multiply_reduce_fusion.1
  651.5 161.1 %while.41 = (s32[]{:T(128)}, f32[2,16,2048]{2,1,0:T(8,128)S(1)}, bf16[2,16,16384]{2,1,0:T(8,128)(2,1)}, bf16[16384,2048]{1,0:T(8,128)(2,1)}, bf16[16384,2048]{1,...) while((s32[]{:T(128)}, f32[2,16,2048]{2,1,0:T(8,128)S(1)}, ...), condition=%wide.region_5.6_spmd.clone, body=%wide.region_4.5_spmd.clone.sunk | while | flops 134479872 | bytes 6422689 | solution.py:86
  654.3 2.1 fusion.66
  659.4 2.1 fusion.66
  664.4 2.1 fusion.66
  813.4 30.0 %fusion.23 = f32[32,1024]{1,0:T(8,128)S(1)} fusion(bf16[32,2048]{1,0:T(8,128)(2,1)S(1)} %bitcast.88, f32[2048,1024]{1,0:T(8,128)} %multiply_reduce_fusion.1), kind=kOutput, calls=%fused_computation.40 | convolution fusion | flops 138412032 | bytes 8650752 | tf_op jit(solution)/shard_map/dot_general | solution.py:62
  843.4 30.2 %fusion.25 = f32[32,1024]{1,0:T(8,128)S(1)} fusion(bf16[32,2048]{1,0:T(8,128)(2,1)S(1)} %bitcast.89, f32[2048,1024]{1,0:T(8,128)} %multiply_reduce_fusion.1), kind=kOutput, calls=%fused_computation.42 | convolution fusion | flops 138412032 | bytes 8650752 | tf_op jit(solution)/shard_map/dot_general | solution.py:63
  874.6 70.5 %all-reduce.2.cloned.1.call-done = f32[2,16,1024]{2,1,0:T(8,128)} async-done(((f32[2,16,1024]{2,1,0:T(8,128)}), f32[2,16,1024]{2,1,0:T(8,128)}) %all-reduce.2.cloned.1.call-update) | async-done | bytes 131088 | tf_op jit(solution)/shard_map/psum | solution.py:122
  946.1 30.2 %fusion.22 = f32[32,2048]{1,0:T(8,128)S(1)} fusion(bf16[32,1024]{1,0:T(8,128)(2,1)S(1)} %bitcast.86, f32[2048,1024]{1,0:T(8,128)} %multiply_reduce_fusion.1), kind=kOutput, calls=%fused_computation.39 | convolution fusion | flops 138412032 | bytes 8716288 | tf_op jit(solution)/shard_map/dot_general | solution.py:62
  976.2 30.4 %fusion.24 = f32[32,2048]{1,0:T(8,128)S(1)} fusion(bf16[32,1024]{1,0:T(8,128)(2,1)S(1)} %bitcast.87, f32[2048,1024]{1,0:T(8,128)} %multiply_reduce_fusion.1), kind=kOutput, calls=%fused_computation.41 | convolution fusion | flops 138412032 | bytes 8716288 | tf_op jit(solution)/shard_map/dot_general | solution.py:63
  1007.4 39.6 %all-gather.5.cloned.1.call-done = bf16[2,16,16384]{2,1,0:T(8,128)(2,1)} async-done(((bf16[2,16,2048]{2,1,0:T(8,128)(2,1)}), bf16[2,16,16384]{2,1,0:T(8,128)(2,1)}) %all-gather.5.cloned.1.call-update) | async-done | bytes 1048592 | tf_op jit(solution)/shard_map/all_gather | solution.py:109
  1047.0 161.2 %while.42 = (s32[]{:T(128)}, f32[2,16,2048]{2,1,0:T(8,128)S(1)}, bf16[2,16,16384]{2,1,0:T(8,128)(2,1)}, bf16[16384,2048]{1,0:T(8,128)(2,1)}, bf16[16384,2048]{1,...) while((s32[]{:T(128)}, f32[2,16,2048]{2,1,0:T(8,128)S(1)}, ...), condition=%wide.region_9.10_spmd.clone, body=%wide.region_8.9_spmd.clone.sunk | while | flops 134545408 | bytes 6422689 | solution.py:86
  1208.2 5.8 psum.15
  (419 shorter events, 362.8 us)
Async XLA Ops:
  7.2 644.3 %all-gather.3.cloned.1.call-start = ((), (), s32[]{:S(2)}) async-start(), calls=%async_computation | async-start | bytes 1179648 | tf_op jit(solution)/shard_map/all_gather | solution.py:109
  9.6 935.5 %all-reduce.2.cloned.1.call-start = ((), (), s32[]{:S(2)}) async-start(), calls=%async_computation.1 | async-start | bytes 262144 | tf_op jit(solution)/shard_map/psum | solution.py:122
  48.4 597.6 %copy-start.2 = (s32[1024]{0:T(1024)S(1)}, s32[1024]{0:T(1024)}, u32[]{:S(2)}) copy-start(s32[1024]{0:T(1024)} %param.15) | copy-start | bytes 12292
  813.4 131.7 %copy-start.1 = (f32[2,16,1024]{2,1,0:T(8,128)S(1)}, f32[2,16,1024]{2,1,0:T(8,128)}, u32[]{:S(2)}) copy-start(f32[2,16,1024]{2,1,0:T(8,128)} %param.16) | copy-start | bytes 393220
  874.3 172.7 %all-gather.5.cloned.1.call-start = ((), (), s32[]{:S(2)}) async-start(), calls=%async_computation.2 | async-start | bytes 1179648 | tf_op jit(solution)/shard_map/all_gather | solution.py:109
  1047.0 161.2 %copy-start = (f32[2,16,2048]{2,1,0:T(8,128)S(1)}, f32[2,16,2048]{2,1,0:T(8,128)}, u32[]{:S(2)}) copy-start(f32[2,16,2048]{2,1,0:T(8,128)} %param.17) | copy-start | bytes 786436
Sparse Core Ops, SparseCore 0:
  10.8 43.2 all-gather.2
  874.5 70.6 all-reduce.1
  1007.5 39.4 all-gather.4
where the time goes:
time: 1230 us; the launch traced here: 1220 us
  other arithmetic  622 us (51%)
  matrix products  384 us (31%)
  waiting for transfers between devices  110 us (9%)
  local copies, waits for them, and re-layouts  49.2 us (4%)
  blocking collectives  38.5 us (3%)
  between operations  13.9 us (1%)
    dynamic_update_slice x32, other arithmetic, build_kernel(): cos_k, sin_k = lax.map(lambda src: kernel_tile(src, pos_loc), sources)  557 us
    dot_general x66, matrix products, apply(): lax.dot_general(stacked, sin_t, dims, preferred_element_type=jnp.float32)  192 us
    dot_general x66, matrix products, apply(): lax.dot_general(stacked, cos_t, dims, preferred_element_type=jnp.float32)  191 us
    psum x1, waiting for transfers between devices, on_device(): farfield = lax.psum(partial_far, 'elem')  70.5 us
    dynamic_slice x64, local copies, waits for them, and re-layouts, slice_panels(): return lax.dynamic_slice_in_dim(piece, begin, block, 2)  49.1 us
    reduce_sum x32, other arithmetic, kernel_tile(): dist = jnp.sum((src[:, :, None] - tgt[:, None, :]) ** 2, axis=0)  39.9 us
    all_gather x2, waiting for transfers between devices, spread(): piece = lax.all_gather(vec, 'elem', axis=2, tiled=True)  39.6 us
    all_gather x1, blocking collectives, on_device(): whole = lax.all_gather(geom, 'elem', axis=1, tiled=True)  32.7 us
  transfers between devices with their start and end apart: 3, of which 2 were waited for; matrix products, arithmetic and copies ran while one was open for 50% of the time, Pallas kernels for 0%

commit v1 on v0

v1 whole, which is shorter than its diff:
```python
import math

import jax
import jax.numpy as jnp
from jax import lax
from jax.experimental import pallas as pl
from jax.experimental.pallas import tpu as pltpu
from jax.sharding import PartitionSpec as P

PANELS = 16384
RBANK = 4096

WAVENUM = 32.0
SOFTEN = 0.0025
TURNS = WAVENUM / (2.0 * math.pi)
MAGIC = 12582912.0

COS = (0.99999921, -19.73898036, 64.92865742, -85.27162153, 58.79049212, -21.07110563)
SIN = (6.28316113, -41.33683183, 81.44770647, -74.9094197, 33.54835515)

f32 = jnp.float32
bf16 = jnp.bfloat16


def positions(angles):
    phi = angles[0]
    psi = angles[1]
    return jnp.stack(
        [4.0 * jnp.cos(psi), jnp.sin(psi) * jnp.cos(phi), 0.6 * jnp.sin(psi) * jnp.sin(phi)]
    )


def weights(counts):
    return counts.astype(f32) * (0.5 / (4.0 * math.sqrt(PANELS)))


def lattice(index, count):
    where = index.astype(f32)
    height = 1.0 - (2.0 * where + 1.0) / count
    radius = jnp.sqrt(1.0 - height * height)
    turn = where * (math.pi * (3.0 - math.sqrt(5.0)))
    return jnp.stack([radius * jnp.cos(turn), radius * jnp.sin(turn), height])


def plane(dvec, pos):
    phase = WAVENUM * jnp.sum(dvec[:, :, None] * pos[:, None, :], axis=0)
    return jnp.stack([jnp.cos(phase), jnp.sin(phase)])


def pieces(x):
    hi = lax.reduce_precision(x, 8, 7)
    mid = lax.reduce_precision(x - hi, 8, 7)
    return hi, mid, (x - hi) - mid


def product_rows(a, b):
    ah, am, al = pieces(a)
    bh, bm, bl = pieces(b)
    left = jnp.concatenate([ah, ah, am, am, ah, al], axis=0)
    right = jnp.concatenate([bh, bm, bh, bm, bl, bh], axis=0)
    return left, right


def pad_rows(x):
    return jnp.pad(x, ((0, 32 - x.shape[0]), (0, 0))).astype(bf16)


def distance_rows(src, tgt):
    left, right = product_rows(-2.0 * src, tgt)
    ones_s = jnp.ones((3, src.shape[1]), f32)
    ones_t = jnp.ones((3, tgt.shape[1]), f32)
    sq_s = jnp.stack(pieces(jnp.sum(src * src, axis=0)))
    sq_t = jnp.stack(pieces(jnp.sum(tgt * tgt, axis=0) + SOFTEN * TURNS * TURNS))
    left = jnp.concatenate([left, sq_s, ones_s], axis=0)
    right = jnp.concatenate([right, ones_t, sq_t], axis=0)
    return pad_rows(left), pad_rows(right)


def horner(coefs, z, scale):
    total = coefs[-1] * scale
    for c in coefs[-2::-1]:
        total = total * z + c * scale
    return total


def green(d2):
    inv = lax.rsqrt(d2)
    t = d2 * inv
    r = t - ((t + MAGIC) - MAGIC)
    z = r * r
    cos_k = horner(COS, z, TURNS) * inv
    sin_k = horner(SIN, z, TURNS) * (r * inv)
    return cos_k.astype(bf16), sin_k.astype(bf16)


def mm(a, b):
    return lax.dot_general(a, b, (((1,), (0,)), ((), ())), preferred_element_type=f32)


def mt(a, b):
    return lax.dot_general(a, b, (((1,), (1,)), ((), ())), preferred_element_type=f32)


def chunk_of(total, most):
    size = min(total, most)
    while total % size:
        size //= 2
    return size


def forward_body(sb, a_ref, b_ref, va_ref, vb_ref, c_ref, s_ref, u_ref):
    count = a_ref.shape[0] // sb

    def make(k):
        rows = pl.ds(pl.multiple_of(k * sb, sb), sb)
        cos_k, sin_k = green(mm(a_ref[rows, :], b_ref[...]))
        c_ref[rows, :] = cos_k
        s_ref[rows, :] = sin_k

    def use(k):
        rows = pl.ds(pl.multiple_of(k * sb, sb), sb)
        return mm(va_ref[:, rows], c_ref[rows, :]) + mm(vb_ref[:, rows], s_ref[rows, :])

    u_ref[...] = jnp.zeros_like(u_ref)
    make(0)

    def body(k, carry):
        u_ref[...] += use(k - 1)
        make(k)
        return carry

    lax.fori_loop(1, count, body, 0)
    u_ref[...] += use(count - 1)


def forward(a, b, va, vb):
    sources = a.shape[0]
    targets = b.shape[1]
    lanes = va.shape[0]
    tb = chunk_of(targets, 256)
    sb = chunk_of(sources, 256)
    whole = lambda x: pl.BlockSpec(x.shape, lambda i: (0, 0))
    col = lambda n: pl.BlockSpec((n, tb), lambda i: (0, i))
    cells = sources * targets
    return pl.pallas_call(
        lambda *refs: forward_body(sb, *refs),
        grid=(targets // tb,),
        in_specs=[whole(a), col(32), whole(va), whole(vb)],
        out_specs=[col(sources), col(sources), col(lanes)],
        out_shape=[
            jax.ShapeDtypeStruct((sources, targets), bf16),
            jax.ShapeDtypeStruct((sources, targets), bf16),
            jax.ShapeDtypeStruct((lanes, targets), f32),
        ],
        compiler_params=pltpu.CompilerParams(vmem_limit_bytes=48 * 2**20),
        cost_estimate=pl.CostEstimate(
            flops=cells * (30 + 4 * lanes), bytes_accessed=4 * cells, transcendentals=cells
        ),
        name="forward",
    )(a, b, va, vb)


def backward_body(ma_ref, mb_ref, c_ref, s_ref, v_ref, g_ref):
    nu = mt(ma_ref[...], c_ref[...]) + mt(mb_ref[...], s_ref[...])
    g_ref[...] = jnp.sum(nu * v_ref[...].astype(f32), axis=0, keepdims=True)


def backward(ma, mb, cos_k, sin_k, v):
    sources, targets = cos_k.shape
    lanes = ma.shape[0]
    sb = chunk_of(sources, 256)
    whole = lambda x: pl.BlockSpec(x.shape, lambda i: (0, 0))
    row = pl.BlockSpec((sb, targets), lambda i: (i, 0))
    col = lambda n: pl.BlockSpec((n, sb), lambda i: (0, i))
    cells = sources * targets
    return pl.pallas_call(
        backward_body,
        grid=(sources // sb,),
        in_specs=[whole(ma), whole(mb), row, row, col(lanes)],
        out_specs=col(1),
        out_shape=jax.ShapeDtypeStruct((1, sources), f32),
        compiler_params=pltpu.CompilerParams(vmem_limit_bytes=48 * 2**20),
        cost_estimate=pl.CostEstimate(
            flops=cells * 4 * lanes, bytes_accessed=4 * cells, transcendentals=0
        ),
        name="backward",
    )(ma, mb, cos_k, sin_k, v)


def table_body(rb, a_ref, b_ref, c_ref, s_ref):
    def body(k, carry):
        rows = pl.ds(pl.multiple_of(k * rb, rb), rb)
        t = mm(a_ref[rows, :], b_ref[...])
        r = t - ((t + MAGIC) - MAGIC)
        z = r * r
        c_ref[rows, :] = horner(COS, z, 1.0).astype(bf16)
        s_ref[rows, :] = (horner(SIN, z, 1.0) * r).astype(bf16)
        return carry

    lax.fori_loop(0, a_ref.shape[0] // rb, body, 0)


def far_table(a, b):
    rows = a.shape[0]
    recv = b.shape[1]
    tb = chunk_of(recv, 256)
    rb = chunk_of(rows, 256)
    col = lambda n: pl.BlockSpec((n, tb), lambda i: (0, i))
    out = jax.ShapeDtypeStruct((rows, recv), bf16)
    cells = rows * recv
    return pl.pallas_call(
        lambda *refs: table_body(rb, *refs),
        grid=(recv // tb,),
        in_specs=[pl.BlockSpec(a.shape, lambda i: (0, 0)), col(32)],
        out_specs=[col(rows), col(rows)],
        out_shape=[out, out],
        compiler_params=pltpu.CompilerParams(vmem_limit_bytes=48 * 2**20),
        cost_estimate=pl.CostEstimate(flops=cells * 30, bytes_accessed=4 * cells, transcendentals=0),
        name="far_table",
    )(a, b)


def apply(vec, cos_t, sin_t, sign, axis):
    half = vec.shape[1]
    stacked = vec.reshape(2 * half, vec.shape[2])
    dims = (((1,), (axis,)), ((), ()))
    first = lax.dot_general(stacked, cos_t, dims, preferred_element_type=f32)
    second = lax.dot_general(stacked, sin_t, dims, preferred_element_type=f32)
    real = first[:half] - sign * second[half:]
    imag = first[half:] + sign * second[:half]
    return jnp.stack([real, imag])


def on_device(panel_angles, impedance, quad_count, receivers, farfield_data, warm_density):
    rows = impedance.shape[0]
    count_dir = farfield_data.shape[1]
    groups = lax.axis_size("dir")
    blocks = lax.axis_size("elem")
    ndir = count_dir * groups
    sub = rows // groups
    lanes = 2 * ndir
    me = lax.axis_index("dir")

    w_loc = weights(quad_count)
    wz_loc = w_loc * impedance
    pos_loc = positions(panel_angles)
    turn_loc = pos_loc * TURNS

    src = lax.dynamic_slice_in_dim(turn_loc, me * sub, sub, 1)
    src = lax.all_gather(src, "elem", axis=1, tiled=True)
    v = (wz_loc * warm_density).astype(bf16)
    v = v.reshape(2, count_dir, groups, sub)
    v = lax.all_to_all(v, "dir", 2, 0, tiled=False)
    v = lax.all_gather(v, "elem", axis=0)
    v = jnp.transpose(v, (1, 2, 3, 0, 4)).reshape(groups, 2, count_dir, blocks * sub)
    va = v.reshape(lanes, blocks * sub)
    vb = jnp.stack([-v[:, 1], v[:, 0]], axis=1).reshape(lanes, blocks * sub)

    left, right = distance_rows(src, turn_loc)
    cos_k, sin_k, image = forward(left.T, right, va, vb)
    image = lax.psum_scatter(
        image.reshape(groups, 2, count_dir, rows), "dir", scatter_dimension=0, tiled=False
    )

    dvec = lattice(me * count_dir + jnp.arange(count_dir, dtype=jnp.int32), ndir)
    state = plane(dvec, pos_loc) - image

    left, right = product_rows(turn_loc, lattice(receivers, RBANK))
    cos_t, sin_t = far_table(pad_rows(left).T, pad_rows(right))
    partial_far = apply((w_loc * state).astype(bf16), cos_t, sin_t, -1.0, 0)
    farfield = lax.psum(partial_far, "elem")
    misfit = (farfield - farfield_data).astype(bf16)
    adjoint = (w_loc * apply(misfit, cos_t, sin_t, 1.0, 1)).astype(bf16)

    mu = lax.all_gather(adjoint, "dir", axis=0)
    ma = mu.reshape(lanes, rows)
    mb = jnp.stack([mu[:, 1], -mu[:, 0]], axis=1).reshape(lanes, rows)
    grad = backward(ma, mb, cos_k, sin_k, va)
    grad = lax.psum_scatter(grad.reshape(blocks, sub), "elem", scatter_dimension=0, tiled=False)
    grad = lax.all_gather(grad, "dir", axis=0, tiled=True)
    return (grad / (-ndir * wz_loc), state)


def solution(mesh):
    placed = (
        P(None, "elem"),
        P("elem"),
        P("elem"),
        P(),
        P(None, "dir", None),
        P(None, "dir", "elem"),
    )
    return jax.shard_map(
        on_device,
        mesh=mesh,
        in_specs=placed,
        out_specs=(P("elem"), P(None, "dir", "elem")),
        check_vma=False,
    )
```

time: 1230 us -> 329 us (0.27)
  other arithmetic: 622 us -> 10 us
  matrix products: 384 us -> 8.96 us
  Pallas kernels: 0 us -> 84.7 us
  blocking collectives: 38.5 us -> 79.2 us
  local copies, waits for them, and re-layouts: 49.2 us -> 10.4 us
    dynamic_update_slice x32 -> x0, other arithmetic: 557 us -> none  [build_kernel(): cos_k, sin_k = lax.map(lambda src: kernel_tile(src, pos_loc), sources)]
    dot_general x132 -> x4, matrix products: 384 us -> 8.96 us  [the longest x2 6.81 us: apply(): first = lax.dot_general(stacked, cos_t, dims, preferred_element_type=f32)]
    pallas_call x0 -> x3, Pallas kernels: none -> 84.7 us  [the longest x1 51.6 us: forward(): pl.pallas_call(lambda *refs: forward_body(sb, *refs), grid=(targets // tb...]
    dynamic_slice x64 -> x1, local copies, waits for them, and re-layouts: 49.1 us -> 0.01 us  [on_device(): src = lax.dynamic_slice_in_dim(turn_loc, me * sub, sub, 1)]
    reduce_sum x34 -> x1, other arithmetic: 44.8 us -> 0.08 us  [distance_rows(): sq_s = jnp.stack(pieces(jnp.sum(src * src, axis=0)))]
    unnamed x0 -> x1, blocking collectives: none -> 35.4 us
    all_gather x1 -> x3, blocking collectives: 32.7 us -> 43.8 us  [the longest x1 31.5 us: on_device(): src = lax.all_gather(src, 'elem', axis=1, tiled=True)]
    all_gather x2 -> x1, waiting for transfers between devices: 39.6 us -> 39.8 us  [on_device(): v = lax.all_gather(v, 'elem', axis=0)]
  transfers between devices with their start and end apart: 3 -> 4, of which waited for: 2 -> 3; matrix products, arithmetic and copies ran while one was open for 50% -> 2% of each run, Pallas kernels for 0% -> 4%
where the time goes in v1:
time: 329 us; the launch traced here: 328 us
  waiting for transfers between devices  117 us (36%)
  Pallas kernels  84.7 us (26%)
  blocking collectives  79.2 us (24%)
  between operations  14.1 us (4%)
  local copies, waits for them, and re-layouts  10.4 us (3%)
  other arithmetic  10 us (3%)
  matrix products  8.96 us (3%)
  starting transfers between devices  4.29 us (1%)
    psum x1, waiting for transfers between devices, on_device(): farfield = lax.psum(partial_far, 'elem')  69.1 us
    pallas_call x1, Pallas kernels, forward(): pl.pallas_call(lambda *refs: forward_body(sb, *refs), grid=(targets // tb...  51.6 us
    all_gather x1, waiting for transfers between devices, on_device(): v = lax.all_gather(v, 'elem', axis=0)  39.8 us
    unnamed x1, blocking collectives  35.4 us
    all_gather x1, blocking collectives, on_device(): src = lax.all_gather(src, 'elem', axis=1, tiled=True)  31.5 us
    pallas_call x1, Pallas kernels, backward(): pl.pallas_call(backward_body, grid=(sources // sb,), in_specs=[whole(ma),...  20.7 us
    pallas_call x1, Pallas kernels, far_table(): pl.pallas_call(lambda *refs: table_body(rb, *refs), grid=(recv // tb,), i...  12.4 us
    reduce_scatter x1, waiting for transfers between devices, on_device(): lax.psum_scatter(image.reshape(groups, 2, count_dir, rows), 'dir', scatte...  7.61 us
  transfers between devices with their start and end apart: 4, of which 3 were waited for; matrix products, arithmetic and copies ran while one was open for 2% of the time, Pallas kernels for 4%

profile of v1, /device:TPU:0, one launch (start us, length us, event | category | flops | bytes accessed | tf_op | source)
XLA Modules:
  0.0 328.2 jit_solution(11789825955949823028)
XLA Ops:
  7.2 0.7 convert_multiply_fusion
  7.9 1.0 multiply_convert_fusion
  8.9 0.1 broadcast_in_dim_reshape.3
  8.9 0.7 copy.39
  9.6 4.2 %all-to-all-start = ((bf16[1,2,16,4,512]{4,2,1,0,3:T(8,128)(2,1)}), bf16[1,2,16,4,512]{4,2,1,0,3:T(8,128)(2,1)S(1)}, u32[]{:S(2)}, u32[]{:S(2)}) async-start(bf16[1,2,16,4,512]{4,2,1,0,3:T(8,128)(2,1)} %copy.39), calls=%async_computation | async-start | bytes 262144 | tf_op jit(solution)/shard_map/all_to_all | solution.py:253
  13.8 1.3 cosine_multiply_fusion.1
  15.1 0.1 pad_maximum_fusion.4
  15.2 31.5 %all_gather.13 = f32[3,4096]{1,0:T(4,128)S(1)} all-gather(f32[3,512]{1,0:T(4,128)S(1)} %constant_dynamic-slice_fusion.1), channel_id=1, replica_groups=mesh['dir'=4,'elem'=8] {'elem'}, dimensions={1}, use_global_device_ids=true | all-gather | bytes 55296 | tf_op jit(solution)/shard_map/all_gather | solution.py:250
  46.7 0.1 multiply_reduce_fusion.1
  46.8 0.6 copy-done.4
  47.6 0.6 concatenate.23
  48.1 0.5 copy.38
  48.7 0.4 concatenate.24
  49.1 0.2 pad_bitcast_fusion.refs_0_
  49.3 39.8 %all-gather.4.cloned.1.call-done = bf16[32,1,2,16,1,512]{5,3,4,2,1,0:T(8,128)(2,1)} async-done(((bf16[4,1,2,16,1,512]{5,3,4,2,1,0:T(8,128)(2,1)}), bf16[32,1,2,16,1,512]{5,3,4,2,1,0:T(8,128)(2,1)}) %all-gather.4.cloned.1.call-update) | async-done | bytes 1048592 | tf_op jit(solution)/shard_map/all_gather | solution.py:254
  89.1 1.4 copy.44
  90.5 0.1 slice_negate_fusion
  90.6 0.6 copy.41
  91.2 0.4 copy.45
  91.6 0.1 pad_maximum_fusion
  91.8 51.6 %forward.1 = (bf16[4096,2048]{1,0:T(8,128)(2,1)}, bf16[4096,2048]{1,0:T(8,128)(2,1)}, f32[128,2048]{1,0:T(8,128)}) custom-call(bf16[4096,32]{1,0:T(8,128)(2,1)S(1)} %pad_bitcast_fusion.refs_0_, bf16[32,2048]{1,0:T(8,128)(2,1)S(1)} %pad.21.refs_1_, bf16[128,4096]{1,0:T(8,128)(2,1)S(1)} %bitcast.60, bf16[128,4096]{1,0:T(8,128)(2,1)S(1)} %bitcast.63), custom_call_target="tpu_custom_call" | custom-call | flops 4546625536 | bytes 33554432 | tf_op jit(solution)/shard_map/forward/pallas_call | solution.py:145
  143.4 0.3 concatenate.25
  143.8 0.3 copy.43
  144.2 0.3 concatenate.26
  144.5 0.1 pad_bitcast_fusion.1.refs_0_
  144.6 12.4 %far_table.1 = (bf16[2048,1024]{1,0:T(8,128)(2,1)S(1)}, bf16[2048,1024]{1,0:T(8,128)(2,1)}) custom-call(bf16[2048,32]{1,0:T(8,128)(2,1)S(1)} %pad_bitcast_fusion.1.refs_0_, bf16[32,1024]{1,0:T(8,128)(2,1)S(1)} %pad.23.refs_1_), custom_call_target="tpu_custom_call" | custom-call | flops 62914560 | bytes 8388608 | tf_op jit(solution)/shard_map/far_table/pallas_call | solution.py:211
  157.0 2.0 copy-done
  159.0 0.1 multiply_reduce_fusion
  159.1 0.5 cosine_bitcast_fusion
  159.6 7.6 %reduce-scatter.2.cloned.1.call-done = f32[1,2,16,2048]{3,2,1,0:T(8,128)} async-done(((f32[4,2,16,2048]{3,2,1,0:T(8,128)}), f32[1,2,16,2048]{3,2,1,0:T(8,128)}) %reduce-scatter.2.cloned.1.call-update) | async-done | bytes 262160 | tf_op jit(solution)/shard_map/reduce_scatter | solution.py:261
  167.2 1.8 bitcast_subtract_fusion
  169.0 1.0 fusion.2
  170.0 3.0 fusion.16
  173.1 0.8 fusion.17
  174.0 0.7 pad_maximum_fusion.3
  174.6 0.6 dynamic-slice
  175.3 69.1 %all-reduce.7.cloned.1.call-done = f32[2,16,1024]{2,1,0:T(8,128)} async-done(((f32[2,16,1024]{2,1,0:T(8,128)}), f32[2,16,1024]{2,1,0:T(8,128)}) %all-reduce.7.cloned.1.call-update) | async-done | bytes 131088 | tf_op jit(solution)/shard_map/psum | solution.py:271
  244.4 1.1 subtract_convert_fusion
  245.5 3.8 %fusion.18 = f32[32,2048]{1,0:T(8,128)S(1)} fusion(bf16[32,1024]{1,0:T(8,128)(2,1)S(1)} %bitcast.68, bf16[2048,1024]{1,0:T(8,128)(2,1)} %copy-done), kind=kOutput, calls=%fused_computation.84 | convolution fusion | flops 134217728 | bytes 4521984 | tf_op jit(solution)/shard_map/dot_general | solution.py:227
  249.2 1.3 fusion.19
  250.6 7.1 %all_gather.15 = bf16[4,2,16,2048]{3,2,1,0:T(8,128)(2,1)S(1)} all-gather(bf16[1,2,16,2048]{3,2,1,0:T(8,128)(2,1)S(1)} %fusion), channel_id=1, replica_groups=mesh['dir'=4,'elem'=8] {'dir'}, dimensions={0}, use_global_device_ids=true | all-gather | bytes 655360 | tf_op jit(solution)/shard_map/all_gather | solution.py:275
  257.9 20.7 %backward.1 = f32[1,4096]{1,0:T(1,128)S(1)} custom-call(bf16[128,2048]{1,0:T(8,128)(2,1)S(1)} %bitcast.59, bf16[128,2048]{1,0:T(8,128)(2,1)S(1)} %bitcast.62, bf16[4096,2048]{1,0:T(8,128)(2,1)} %get-tuple-element.10.c_ref, bf16[4096,2048]{1,0:T(8,128)(2,1)} %get-tuple-element.11.s_ref, bf16[128,4096]{1,0:T(8,128)(2,1)S(1)} %bitcast.61), custom_call_target="tpu_custom_call" | custom-call | flops 4294967296 | bytes 33554432 | tf_op jit(solution)/shard_map/backward/pallas_call | solution.py:176
  278.6 0.5 broadcast.209
  279.1 0.7 reduce.3
  279.8 35.4 %all-reduce.4 = f32[8,512]{1,0:T(8,128)S(1)} all-reduce(f32[8,512]{1,0:T(8,128)S(1)} %reshape.195), channel_id=5, replica_groups=mesh['dir'=4,'elem'=8] {'elem'}, use_global_device_ids=true, to_apply=%region_5.6.clone | all-reduce | flops 4096 | bytes 32768
  315.3 0.6 constant_dynamic-slice_fusion
  315.9 5.2 %all-gather.1 = f32[1,2048]{1,0:T(1,128)S(1)} all-gather(f32[1,512]{1,0:T(1,128)S(1)} %constant_dynamic-slice_fusion), channel_id=3, replica_groups=mesh['dir'=4,'elem'=8] {'dir'}, dimensions={1}, use_global_device_ids=true | all-gather | bytes 10240 | tf_op jit(solution)/shard_map/all_gather | solution.py:280
  321.1 0.6 multiply_divide_fusion
  (40 shorter events, 0.6 us)
Async XLA Ops:
  9.6 37.1 %all-to-all-start = ((bf16[1,2,16,4,512]{4,2,1,0,3:T(8,128)(2,1)}), bf16[1,2,16,4,512]{4,2,1,0,3:T(8,128)(2,1)S(1)}, u32[]{:S(2)}, u32[]{:S(2)}) async-start(bf16[1,2,16,4,512]{4,2,1,0,3:T(8,128)(2,1)} %copy.39), calls=%async_computation | async-start | bytes 262144 | tf_op jit(solution)/shard_map/all_to_all | solution.py:253
  13.8 75.3 %all-gather.4.cloned.1.call-start = ((), (), s32[]{:S(2)}) async-start(), calls=%async_computation.4 | async-start | bytes 1179648 | tf_op jit(solution)/shard_map/all_gather | solution.py:254
  46.8 0.7 copy-start.4
  47.4 119.8 %reduce-scatter.2.cloned.1.call-start = ((), (), s32[]{:S(2)}) async-start(), calls=%async_computation.2 | async-start | bytes 1310720 | tf_op jit(solution)/shard_map/reduce_scatter | solution.py:261
  89.1 1.5 copy-start.3
  91.8 52.3 %copy-start.6 = (s32[1024]{0:T(1024)S(1)}, s32[1024]{0:T(1024)}, u32[]{:S(2)}) copy-start(s32[1024]{0:T(1024)} %param.9) | copy-start | bytes 12292
  143.4 101.0 %all-reduce.7.cloned.1.call-start = ((), (), s32[]{:S(2)}) async-start(), calls=%async_computation.3 | async-start | bytes 262144 | tf_op jit(solution)/shard_map/psum | solution.py:271
  157.0 2.0 copy-start
  167.2 5.9 %copy-start.1 = (bf16[2048,1024]{1,0:T(8,128)(2,1)S(1)}, bf16[2048,1024]{1,0:T(8,128)(2,1)}, u32[]{:S(2)}) copy-start(bf16[2048,1024]{1,0:T(8,128)(2,1)} %get-tuple-element.9) | copy-start | bytes 12582916
  170.0 4.6 %copy-start.7 = (u32[32]{0:T(128)S(1)}, u32[32]{0:T(128)}, u32[]{:S(2)}) copy-start(u32[32]{0:T(128)} %constant.65) | copy-start | bytes 388
  170.0 74.4 %copy-start.5 = (f32[2,16,1024]{2,1,0:T(8,128)S(1)}, f32[2,16,1024]{2,1,0:T(8,128)}, u32[]{:S(2)}) copy-start(f32[2,16,1024]{2,1,0:T(8,128)} %param.10) | copy-start | bytes 393220
  244.4 4.8 %copy-start.2 = (bf16[2048,1024]{1,0:T(8,128)(2,1)S(1)}, bf16[2048,1024]{1,0:T(8,128)(2,1)}, u32[]{:S(2)}) copy-start(bf16[2048,1024]{1,0:T(8,128)(2,1)} %get-tuple-element.9) | copy-start | bytes 12582916
Sparse Core Ops, SparseCore 0:
  47.6 41.4 all-gather.3
  143.5 23.6 reduce-scatter.1
  174.8 69.5 all-reduce.6

commit v2 on v1

--- a/solution.py
+++ b/solution.py
@@ -108,83 +108,350 @@
     return size
 
 
-def forward_body(sb, a_ref, b_ref, va_ref, vb_ref, c_ref, s_ref, u_ref):
-    count = a_ref.shape[0] // sb
-
-    def make(k):
-        rows = pl.ds(pl.multiple_of(k * sb, sb), sb)
-        cos_k, sin_k = green(mm(a_ref[rows, :], b_ref[...]))
-        c_ref[rows, :] = cos_k
-        s_ref[rows, :] = sin_k
-
-    def use(k):
-        rows = pl.ds(pl.multiple_of(k * sb, sb), sb)
-        return mm(va_ref[:, rows], c_ref[rows, :]) + mm(vb_ref[:, rows], s_ref[rows, :])
-
+def peers_of(name):
+    me = lax.axis_index(name)
+    size = lax.axis_size(name)
+    return [lax.rem(me + step, size) for step in range(1, size)]
+
+
+def meet(*names):
+    barrier = pltpu.get_barrier_semaphore()
+    total = 0
+    for name in names:
+        for peer in peers_of(name):
+            pl.semaphore_signal(
+                barrier, inc=1, device_id={name: peer}, device_id_type=pl.DeviceIdType.MESH
+            )
+            total += 1
+    pl.semaphore_wait(barrier, total)
+
+
+def push(src, dst, send, recv, name, peer):
+    return pltpu.make_async_remote_copy(
+        src_ref=src,
+        dst_ref=dst,
+        send_sem=send,
+        recv_sem=recv,
+        device_id={name: peer},
+        device_id_type=pl.DeviceIdType.MESH,
+    )
+
+
+def params(collective_id):
+    return pltpu.CompilerParams(
+        collective_id=collective_id, has_side_effects=True, vmem_limit_bytes=56 * 2**20
+    )
+
+
+VM = pl.BlockSpec(memory_space=pltpu.VMEM)
+HBM = pl.BlockSpec(memory_space=pl.ANY)
+DMA = pltpu.SemaphoreType.DMA
+
+
+def gather_body(name, x_ref, o_ref, send, recv):
+    me = lax.axis_index(name)
+    o_ref[me] = x_ref[...]
+    meet(name)
+    for peer in peers_of(name):
+        push(x_ref, o_ref.at[me], send.at[peer], recv.at[me], name, peer).start()
+    for peer in peers_of(name):
+        done = push(x_ref, o_ref.at[peer], send.at[peer], recv.at[peer], name, peer)
+        done.wait_send()
+        done.wait_recv()
+
+
+def gather(x, name, size, collective_id):
+    return pl.pallas_call(
+        lambda *refs: gather_body(name, *refs),
+        in_specs=[VM],
+        out_specs=VM,
+        out_shape=jax.ShapeDtypeStruct((size, *x.shape), x.dtype),
+        scratch_shapes=[DMA((size,)), DMA((size,))],
+        compiler_params=params(collective_id),
+        name="gather_" + name,
+    )(x)
+
+
+def forward_body(
+    a_ref, b_ref, v_ref,
+    c_out, s_out, vg_ref, image_ref,
+    c_ref, s_ref, part_ref, vb_ref, u_ref, ur_ref,
+    send_a, recv_a, send_b, recv_b, send_u, recv_u, sem_c, sem_s,
+):
+    blocks, sub = a_ref.shape[:2]
+    nb, _, tb = b_ref.shape
+    groups, pair = v_ref.shape[:2]
+    half = pair // 2
+    lanes = groups * pair
+    lag = nb // 2
+    me = lax.axis_index("dir")
+    spot = lax.axis_index("elem")
+
+    def make(j, e):
+        cos_k, sin_k = green(mm(a_ref[e], b_ref[j]))
+        c_ref[j, e] = cos_k
+        s_ref[j, e] = sin_k
+
+    def use(j, e):
+        va = vg_ref[e].reshape(lanes, sub)
+        vb = vb_ref[e].reshape(lanes, sub)
+        u_ref[j] += (mm(va, c_ref[j, e]) + mm(vb, s_ref[j, e])).reshape(groups, pair, tb)
+
+    def start_out(j):
+        pltpu.make_async_copy(c_ref.at[j], c_out.at[j], sem_c.at[j]).start()
+        pltpu.make_async_copy(s_ref.at[j], s_out.at[j], sem_s.at[j]).start()
+
+    def send_block(j):
+        for peer in peers_of("dir"):
+            push(
+                u_ref.at[j, peer], ur_ref.at[me, j],
+                send_u.at[peer, j], recv_u.at[me, j], "dir", peer,
+            ).start()
+
+    def make_only(j, carry):
+        lax.fori_loop(0, blocks, lambda e, c: (make(j, e), c)[1], 0)
+        start_out(j)
+        return carry
+
+    def both(j, carry):
+        def inner(e, c):
+            use(j - lag, e)
+            make(j, e)
+            return c
+
+        lax.fori_loop(0, blocks, inner, 0)
+        start_out(j)
+        send_block(j - lag)
+        return carry
+
+    def use_only(j, carry):
+        lax.fori_loop(0, blocks, lambda e, c: (use(j, e), c)[1], 0)
+        send_block(j)
+        return carry
+
+    part_ref[me] = v_ref[me]
+    meet("dir", "elem")
+    for peer in peers_of("dir"):
+        push(
+            v_ref.at[peer], part_ref.at[me], send_a.at[peer], recv_a.at[me], "dir", peer
+        ).start()
     u_ref[...] = jnp.zeros_like(u_ref)
-    make(0)
-
-    def body(k, carry):
-        u_ref[...] += use(k - 1)
-        make(k)
-        return carry
-
-    lax.fori_loop(1, count, body, 0)
-    u_ref[...] += use(count - 1)
-
-
-def forward(a, b, va, vb):
-    sources = a.shape[0]
-    targets = b.shape[1]
-    lanes = va.shape[0]
-    tb = chunk_of(targets, 256)
-    sb = chunk_of(sources, 256)
-    whole = lambda x: pl.BlockSpec(x.shape, lambda i: (0, 0))
-    col = lambda n: pl.BlockSpec((n, tb), lambda i: (0, i))
-    cells = sources * targets
+    make_only(0, 0)
+    for peer in peers_of("dir"):
+        done = push(
+            v_ref.at[peer], part_ref.at[peer], send_a.at[peer], recv_a.at[peer], "dir", peer
+        )
+        done.wait_send()
+        done.wait_recv()
+    vg_ref[spot] = part_ref[...]
+    for peer in peers_of("elem"):
+        push(
+            part_ref, vg_ref.at[spot], send_b.at[peer], recv_b.at[spot], "elem", peer
+        ).start()
+    lax.fori_loop(1, lag, make_only, 0)
+    for peer in peers_of("elem"):
+        done = push(
+            part_ref, vg_ref.at[peer], send_b.at[peer], recv_b.at[peer], "elem", peer
+        )
+        done.wait_send()
+        done.wait_recv()
+    vb_ref[:, :, :half] = -vg_ref[:, :, half:]
+    vb_ref[:, :, half:] = vg_ref[:, :, :half]
+
+    lax.fori_loop(lag, nb, both, 0)
+    lax.fori_loop(nb - lag, nb, use_only, 0)
+
+    for j in range(nb):
+        total = u_ref[j, me]
+        for peer in peers_of("dir"):
+            done = push(
+                u_ref.at[j, peer], ur_ref.at[peer, j],
+                send_u.at[peer, j], recv_u.at[peer, j], "dir", peer,
+            )
+            done.wait_send()
+            done.wait_recv()
+            total += ur_ref[peer, j]
+        image_ref[:, j * tb : (j + 1) * tb] = total
+    for j in range(nb):
+        pltpu.make_async_copy(c_ref.at[j], c_out.at[j], sem_c.at[j]).wait()
+        pltpu.make_async_copy(s_ref.at[j], s_out.at[j], sem_s.at[j]).wait()
+
+
+def forward(a, b, v):
+    blocks, sub = a.shape[:2]
+    nb, _, tb = b.shape
+    groups, pair = v.shape[:2]
+    table = (nb, blocks, sub, tb)
+    cells = nb * blocks * sub * tb
     return pl.pallas_call(
-        lambda *refs: forward_body(sb, *refs),
-        grid=(targets // tb,),
-        in_specs=[whole(a), col(32), whole(va), whole(vb)],
-        out_specs=[col(sources), col(sources), col(lanes)],
+        forward_body,
+        in_specs=[VM, VM, VM],
+        out_specs=[HBM, HBM, VM, VM],
         out_shape=[
-            jax.ShapeDtypeStruct((sources, targets), bf16),
-            jax.ShapeDtypeStruct((sources, targets), bf16),
-            jax.ShapeDtypeStruct((lanes, targets), f32),
+            jax.ShapeDtypeStruct(table, bf16),
+            jax.ShapeDtypeStruct(table, bf16),
+            jax.ShapeDtypeStruct((blocks, groups, pair, sub), bf16),
+            jax.ShapeDtypeStruct((pair, nb * tb), f32),
         ],
-        compiler_params=pltpu.CompilerParams(vmem_limit_bytes=48 * 2**20),
+        scratch_shapes=[
+            pltpu.VMEM(table, bf16),
+            pltpu.VMEM(table, bf16),
+            pltpu.VMEM((groups, pair, sub), bf16),
+            pltpu.VMEM((blocks, groups, pair, sub), bf16),
+            pltpu.VMEM((nb, groups, pair, tb), f32),
+            pltpu.VMEM((groups, nb, pair, tb), f32),
+            DMA((groups,)),
+            DMA((groups,)),
+            DMA((blocks,)),
+            DMA((blocks,)),
+            DMA((groups, nb)),
+            DMA((groups, nb)),
+            DMA((nb,)),
+            DMA((nb,)),
+        ],
+        compiler_params=params(1),
         cost_estimate=pl.CostEstimate(
-            flops=cells * (30 + 4 * lanes), bytes_accessed=4 * cells, transcendentals=cells
+            flops=cells * 4 * groups * pair, bytes_accessed=4 * cells, transcendentals=cells
         ),
         name="forward",
-    )(a, b, va, vb)
-
-
-def backward_body(ma_ref, mb_ref, c_ref, s_ref, v_ref, g_ref):
-    nu = mt(ma_ref[...], c_ref[...]) + mt(mb_ref[...], s_ref[...])
-    g_ref[...] = jnp.sum(nu * v_ref[...].astype(f32), axis=0, keepdims=True)
-
-
-def backward(ma, mb, cos_k, sin_k, v):
-    sources, targets = cos_k.shape
-    lanes = ma.shape[0]
-    sb = chunk_of(sources, 256)
-    whole = lambda x: pl.BlockSpec(x.shape, lambda i: (0, 0))
-    row = pl.BlockSpec((sb, targets), lambda i: (i, 0))
-    col = lambda n: pl.BlockSpec((n, sb), lambda i: (0, i))
-    cells = sources * targets
+    )(a, b, v)
+
+
+def backward_body(
+    mu_ref, c_ref, s_ref, v_ref,
+    o_ref,
+    ma_ref, mb_ref, g_ref, gr_ref, all_ref,
+    send_m, recv_m, send_g, recv_g, send_o, recv_o,
+):
+    e = pl.program_id(0)
+    blocks = pl.num_programs(0)
+    groups, pair = ma_ref.shape[:2]
+    half = pair // 2
+    lanes = groups * pair
+    nb, _, sub, tb = c_ref.shape
+    me = lax.axis_index("dir")
+    spot = lax.axis_index("elem")
+
+    @pl.when(e == 0)
+    def _():
+        ma_ref[me] = mu_ref[...]
+        meet("dir", "elem")
+        for peer in peers_of("dir"):
+            push(mu_ref, ma_ref.at[me], send_m.at[peer], recv_m.at[me], "dir", peer).start()
+        for peer in peers_of("dir"):
+            done = push(
+                mu_ref, ma_ref.at[peer], send_m.at[peer], recv_m.at[peer], "dir", peer
+            )
+            done.wait_send()
+            done.wait_recv()
+        mb_ref[:, :half] = ma_ref[:, half:]
+        mb_ref[:, half:] = -ma_ref[:, :half]
+
+    nu = jnp.zeros((lanes, sub), f32)
+    for j in range(nb):
+        cols = slice(j * tb, (j + 1) * tb)
+        nu += mt(ma_ref[:, :, cols].reshape(lanes, tb), c_ref[j, 0])
+        nu += mt(mb_ref[:, :, cols].reshape(lanes, tb), s_ref[j, 0])
+    v = v_ref[0].reshape(lanes, sub).astype(f32)
+    g_ref[e] = jnp.broadcast_to(jnp.sum(nu * v, axis=0, keepdims=True), (8, sub))
+
+    @pl.when(e == blocks - 1)
+    def _():
+        gr_ref[spot] = g_ref[spot]
+        for peer in peers_of("elem"):
+            push(
+                g_ref.at[peer], gr_ref.at[spot], send_g.at[peer], recv_g.at[spot], "elem", peer
+            ).start()
+        for peer in peers_of("elem"):
+            done = push(
+                g_ref.at[peer], gr_ref.at[peer], send_g.at[peer], recv_g.at[peer], "elem", peer
+            )
+            done.wait_send()
+            done.wait_recv()
+        all_ref[me] = jnp.sum(gr_ref[...], axis=0)
+        for peer in peers_of("dir"):
+            push(
+                all_ref.at[me], all_ref.at[me], send_o.at[peer], recv_o.at[me], "dir", peer
+            ).start()
+        for peer in peers_of("dir"):
+            done = push(
+                all_ref.at[me], all_ref.at[peer], send_o.at[peer], recv_o.at[peer], "dir", peer
+            )
+            done.wait_send()
+            done.wait_recv()
+        o_ref[...] = all_ref[...]
+
+
+def backward(mu, cos_k, sin_k, v):
+    nb, blocks, sub, tb = cos_k.shape
+    groups, pair = v.shape[1:3]
+    table = pl.BlockSpec((nb, 1, sub, tb), lambda e: (0, e, 0, 0))
+    cells = cos_k.size
     return pl.pallas_call(
         backward_body,
-        grid=(sources // sb,),
-        in_specs=[whole(ma), whole(mb), row, row, col(lanes)],
-        out_specs=col(1),
-        out_shape=jax.ShapeDtypeStruct((1, sources), f32),
-        compiler_params=pltpu.CompilerParams(vmem_limit_bytes=48 * 2**20),
+        grid=(blocks,),
+        in_specs=[VM, table, table, pl.BlockSpec((1, *v.shape[1:]), lambda e: (e, 0, 0, 0))],
+        out_specs=VM,
+        out_shape=jax.ShapeDtypeStruct((groups, 8, sub), f32),
+        scratch_shapes=[
+            pltpu.VMEM((groups, *mu.shape), bf16),
+            pltpu.VMEM((groups, *mu.shape), bf16),
+            pltpu.VMEM((blocks, 8, sub), f32),
+            pltpu.VMEM((blocks, 8, sub), f32),
+            pltpu.VMEM((groups, 8, sub), f32),
+            DMA((groups,)),
+            DMA((groups,)),
+            DMA((blocks,)),
+            DMA((blocks,)),
+            DMA((groups,)),
+            DMA((groups,)),
+        ],
+        compiler_params=params(2),
         cost_estimate=pl.CostEstimate(
-            flops=cells * 4 * lanes, bytes_accessed=4 * cells, transcendentals=0
+            flops=cells * 4 * groups * pair, bytes_accessed=4 * cells, transcendentals=0
         ),
         name="backward",
-    )(ma, mb, cos_k, sin_k, v)
+    )(mu, cos_k, sin_k, v)
+
+
+def misfit_body(x_ref, data_ref, o_ref, got_ref, send_x, recv_x, send_o, recv_o):
+    me = lax.axis_index("elem")
+    got_ref[me] = x_ref[me]
+    meet("elem")
+    for peer in peers_of("elem"):
+        push(
+            x_ref.at[peer], got_ref.at[me], send_x.at[peer], recv_x.at[me], "elem", peer
+        ).start()
+    for peer in peers_of("elem"):
+        done = push(
+            x_ref.at[peer], got_ref.at[peer], send_x.at[peer], recv_x.at[peer], "elem", peer
+        )
+        done.wait_send()
+        done.wait_recv()
+    o_ref[me] = (jnp.sum(got_ref[...], axis=0) - data_ref[me]).astype(bf16)
+    for peer in peers_of("elem"):
+        push(
+            o_ref.at[me], o_ref.at[me], send_o.at[peer], recv_o.at[me], "elem", peer
+        ).start()
+    for peer in peers_of("elem"):
+        done = push(
+            o_ref.at[me], o_ref.at[peer], send_o.at[peer], recv_o.at[peer], "elem", peer
+        )
+        done.wait_send()
+        done.wait_recv()
+
+
+def far_misfit(x, data):
+    blocks = x.shape[0]
+    return pl.pallas_call(
+        misfit_body,
+        in_specs=[VM, VM],
+        out_specs=VM,
+        out_shape=jax.ShapeDtypeStruct(x.shape, bf16),
+        scratch_shapes=[pltpu.VMEM(x.shape, f32)] + [DMA((blocks,))] * 4,
+        compiler_params=params(3),
+        name="far_misfit",
+    )(x, data)
 
 
 def table_body(rb, a_ref, b_ref, c_ref, s_ref):
@@ -238,7 +505,6 @@
     blocks = lax.axis_size("elem")
     ndir = count_dir * groups
     sub = rows // groups
-    lanes = 2 * ndir
     me = lax.axis_index("dir")
 
     w_loc = weights(quad_count)
@@ -247,20 +513,17 @@
     turn_loc = pos_loc * TURNS
 
     src = lax.dynamic_slice_in_dim(turn_loc, me * sub, sub, 1)
-    src = lax.all_gather(src, "elem", axis=1, tiled=True)
+    src = gather(jnp.pad(src, ((0, 5), (0, 0))), "elem", blocks, 0)
+    src = jnp.transpose(src[:, :3], (1, 0, 2)).reshape(3, blocks * sub)
     v = (wz_loc * warm_density).astype(bf16)
-    v = v.reshape(2, count_dir, groups, sub)
-    v = lax.all_to_all(v, "dir", 2, 0, tiled=False)
-    v = lax.all_gather(v, "elem", axis=0)
-    v = jnp.transpose(v, (1, 2, 3, 0, 4)).reshape(groups, 2, count_dir, blocks * sub)
-    va = v.reshape(lanes, blocks * sub)
-    vb = jnp.stack([-v[:, 1], v[:, 0]], axis=1).reshape(lanes, blocks * sub)
+    v = jnp.transpose(v.reshape(2 * count_dir, groups, sub), (1, 0, 2))
 
     left, right = distance_rows(src, turn_loc)
-    cos_k, sin_k, image = forward(left.T, right, va, vb)
-    image = lax.psum_scatter(
-        image.reshape(groups, 2, count_dir, rows), "dir", scatter_dimension=0, tiled=False
-    )
+    tb = chunk_of(rows, 256)
+    left = left.T.reshape(blocks, sub, left.shape[0])
+    right = jnp.transpose(right.reshape(right.shape[0], rows // tb, tb), (1, 0, 2))
+    cos_k, sin_k, v_all, image = forward(left, right, v)
+    image = image.reshape(2, count_dir, rows)
 
     dvec = lattice(me * count_dir + jnp.arange(count_dir, dtype=jnp.int32), ndir)
     state = plane(dvec, pos_loc) - image
@@ -268,17 +531,18 @@
     left, right = product_rows(turn_loc, lattice(receivers, RBANK))
     cos_t, sin_t = far_table(pad_rows(left).T, pad_rows(right))
     partial_far = apply((w_loc * state).astype(bf16), cos_t, sin_t, -1.0, 0)
-    farfield = lax.psum(partial_far, "elem")
-    misfit = (farfield - farfield_data).astype(bf16)
+    pair = 2 * count_dir
+    recv = farfield_data.shape[2]
+
+    def split(x):
+        return jnp.transpose(x.reshape(pair, blocks, recv // blocks), (1, 0, 2))
+
+    misfit = far_misfit(split(partial_far), split(farfield_data))
+    misfit = jnp.transpose(misfit, (1, 0, 2)).reshape(2, count_dir, recv)
     adjoint = (w_loc * apply(misfit, cos_t, sin_t, 1.0, 1)).astype(bf16)
 
-    mu = lax.all_gather(adjoint, "dir", axis=0)
-    ma = mu.reshape(lanes, rows)
-    mb = jnp.stack([mu[:, 1], -mu[:, 0]], axis=1).reshape(lanes, rows)
-    grad = backward(ma, mb, cos_k, sin_k, va)
-    grad = lax.psum_scatter(grad.reshape(blocks, sub), "elem", scatter_dimension=0, tiled=False)
-    grad = lax.all_gather(grad, "dir", axis=0, tiled=True)
-    return (grad / (-ndir * wz_loc), state)
+    grad = backward(adjoint.reshape(pair, rows), cos_k, sin_k, v_all)
+    return (grad[:, 0].reshape(rows) / (-ndir * wz_loc), state)
 
 
 def solution(mesh):

time: 329 us -> 159 us (0.48)
  waiting for transfers between devices: 117 us -> 0 us
  blocking collectives: 79.2 us -> 0 us
  Pallas kernels: 84.7 us -> 135 us
  between operations: 14.1 us -> 0.91 us
  starting transfers between devices: 4.29 us -> 0 us
  matrix products: 8.96 us -> 5.32 us
    psum x1 -> x0, waiting for transfers between devices: 69.1 us -> none  [on_device(): farfield = lax.psum(partial_far, 'elem')]
    pallas_call x2 -> x4, Pallas kernels: 72.3 us -> 122 us  [the longest x1 59.2 us: forward(): pl.pallas_call(forward_body, in_specs=[VM, VM, VM], out_specs=[HBM, HBM,...]
    all_gather x3 -> x0, blocking collectives: 43.8 us -> none  [the longest x1 31.5 us: on_device(): src = lax.all_gather(src, 'elem', axis=1, tiled=True)]
    all_gather x1 -> x0, waiting for transfers between devices: 39.8 us -> none  [on_device(): v = lax.all_gather(v, 'elem', axis=0)]
    unnamed x1 -> x0, blocking collectives: 35.4 us -> none
    reduce_scatter x1 -> x0, waiting for transfers between devices: 7.61 us -> none  [on_device(): lax.psum_scatter(image.reshape(groups, 2, count_dir, rows), 'dir', scatte...]
    all_to_all x1 -> x0, starting transfers between devices: 4.21 us -> none  [on_device(): v = lax.all_to_all(v, 'dir', 2, 0, tiled=False)]
    dot_general x2, matrix products: 6.81 us -> 3.15 us  [apply(): first = lax.dot_general(stacked, cos_t, dims, preferred_element_type=f32)]
  transfers between devices with their start and end apart: 4 -> 0, of which waited for: 3 -> 0; matrix products, arithmetic and copies ran while one was open for 2% -> 0% of each run, Pallas kernels for 4% -> 0%
where the time goes in v2:
time: 159 us
  Pallas kernels  135 us (85%)
  local copies, waits for them, and re-layouts  9.11 us (6%)
  other arithmetic  8.83 us (6%)
  matrix products  5.32 us (3%)
    pallas_call x1, Pallas kernels, forward(): pl.pallas_call(forward_body, in_specs=[VM, VM, VM], out_specs=[HBM, HBM,...  59.2 us
    pallas_call x1, Pallas kernels, backward(): pl.pallas_call(backward_body, grid=(blocks,), in_specs=[VM, table, table,...  31.4 us
    pallas_call x1, Pallas kernels, far_misfit(): pl.pallas_call(misfit_body, in_specs=[VM, VM], out_specs=VM, out_shape=ja...  20.9 us
    pallas_call x1, Pallas kernels, far_table(): pl.pallas_call(lambda *refs: table_body(rb, *refs), grid=(recv // tb,), i...  12.4 us
    pallas_call x1, Pallas kernels, gather(): pl.pallas_call(lambda *refs: gather_body(name, *refs), in_specs=[VM], out...  10.7 us

profile of v2, /device:TPU:0, one launch (start us, length us, event | category | flops | bytes accessed | tf_op | source)
XLA Modules:
  0.0 158.8 jit_solution(14137719764895496854)
XLA Ops:
  0.6 1.3 cosine_multiply_fusion.1
  1.9 0.1 pad_maximum_fusion.3
  2.0 0.6 pad.24.refs_0_
  2.6 10.7 %gather_elem.1 = f32[8,8,512]{2,1,0:T(8,128)} custom-call(f32[8,512]{1,0:T(8,128)} %pad.24.refs_0_), custom_call_target="tpu_custom_call" | custom-call | tf_op jit(solution)/shard_map/gather_elem/pallas_call | solution.py:164
  13.3 1.0 multiply_reduce_fusion.1
  14.4 0.6 concatenate.16
  15.0 1.4 copy.38
  16.4 0.4 concatenate.17
  16.8 0.7 copy.62
  17.5 0.7 convert_multiply_fusion
  18.2 1.0 multiply_convert_fusion
  19.2 0.1 reshape.173
  19.3 0.7 copy.65
  19.9 0.0 copy-start.4
  19.9 59.2 %forward.1 = (bf16[8,8,512,256]{3,2,1,0:T(8,128)(2,1)}, bf16[8,8,512,256]{3,2,1,0:T(8,128)(2,1)}, bf16[8,4,32,512]{3,2,1,0:T(8,128)(2,1)}, f32[32,2048]{1,0:T(8,128)}) custom-call(bf16[8,512,32]{2,1,0:T(8,128)(2,1)} %bitcast.80, bf16[8,32,256]{2,1,0:T(8,128)(2,1)} %bitcast.90, bf16[4,32,512]{2,1,0:T(8,128)(2,1)} %bitcast.91), custom_call_target="tpu_custom_call" | custom-call | flops 4294967296 | bytes 33554432 | tf_op jit(solution)/shard_map/forward/pallas_call | solution.py:286
  79.2 0.1 multiply_reduce_fusion
  79.3 0.5 cosine_bitcast_fusion
  79.8 1.7 %fusion.21 = (f32[2,16,2048]{2,1,0:T(8,128)}, f32[2,16,2048]{2,1,0:T(8,128)S(1)}) fusion(f32[2,16,2048]{2,1,0:T(8,128)} %bitcast.81, f32[1,16,2048]{2,1,0:T(8,128)S(1)} %get-tuple-element.21, f32[1,16,2048]{2,1,0:T(8,128)S(1)} %get-tuple-element.20), kind=kLoop, calls=%fused_computation.86 | loop fusion | flops 131072 | bytes 1048576 | tf_op jit(solution)/shard_map/sub | solution.py:529
  81.5 1.0 fusion.2
  82.5 0.3 concatenate.18
  82.8 0.3 copy.41
  83.1 0.1 pad_bitcast_fusion.refs_0_
  83.2 0.0 copy-done.4
  83.3 0.3 concatenate.19
  83.6 12.4 %far_table.1 = (bf16[2048,1024]{1,0:T(8,128)(2,1)S(1)}, bf16[2048,1024]{1,0:T(8,128)(2,1)}) custom-call(bf16[2048,32]{1,0:T(8,128)(2,1)S(1)} %pad_bitcast_fusion.refs_0_, bf16[32,1024]{1,0:T(8,128)(2,1)S(1)} %pad.28.refs_1_), custom_call_target="tpu_custom_call" | custom-call | flops 62914560 | bytes 8388608 | tf_op jit(solution)/shard_map/far_table/pallas_call | solution.py:478
  96.0 0.0 copy-start
  96.0 0.0 copy-start.3
  96.0 0.8 fusion.22
  96.8 1.4 copy-done
  98.2 0.8 fusion.23
  99.1 0.7 copy.64
  99.8 0.0 copy-done.3
  99.8 0.7 copy.63
  100.5 20.9 %far_misfit.1 = bf16[8,32,128]{2,1,0:T(8,128)(2,1)} custom-call(f32[8,32,128]{2,1,0:T(8,128)} %bitcast.83, f32[8,32,128]{2,1,0:T(8,128)} %bitcast.85), custom_call_target="tpu_custom_call" | custom-call | tf_op jit(solution)/shard_map/far_misfit/pallas_call | solution.py:446
  121.4 0.0 copy-start.1
  121.4 0.0 copy-start.2
  121.4 2.3 %fusion.8 = f32[32,2048]{1,0:T(8,128)S(1)} fusion(bf16[2048,1024]{1,0:T(8,128)(2,1)S(1)} %get-tuple-element.9, bf16[8,32,128]{2,1,0:T(8,128)(2,1)} %far_misfit.1), kind=kOutput, calls=%fused_computation.29 | convolution fusion | flops 134217728 | bytes 4521984 | tf_op jit(solution)/shard_map/dot_general | solution.py:494
  123.7 0.0 copy-done.1
  123.7 0.0 copy-done.2
  123.8 1.3 fusion.6
  125.2 0.7 fusion.mu_ref
  125.8 31.4 %backward.1 = f32[4,8,512]{2,1,0:T(8,128)} custom-call(bf16[32,2048]{1,0:T(8,128)(2,1)} %fusion.mu_ref, bf16[8,8,512,256]{3,2,1,0:T(8,128)(2,1)} %get-tuple-element.11.c_ref, bf16[8,8,512,256]{3,2,1,0:T(8,128)(2,1)} %get-tuple-element.12.s_ref, bf16[8,4,32,512]{3,2,1,0:T(8,128)(2,1)} %get-tuple-element.13.v_ref), custom_call_target="tpu_custom_call" | custom-call | flops 4294967296 | bytes 33554432 | tf_op jit(solution)/shard_map/backward/pallas_call | solution.py:390
  157.3 0.8 slice.47
  158.1 0.6 multiply_divide_fusion
  (22 shorter events, 0.5 us)
Async XLA Ops:
  19.9 63.3 %copy-start.4 = (s32[1024]{0:T(1024)S(1)}, s32[1024]{0:T(1024)}, u32[]{:S(2)}) copy-start(s32[1024]{0:T(1024)} %param.9) | copy-start | bytes 12292
  96.0 2.2 %copy-start = (bf16[2048,1024]{1,0:T(8,128)(2,1)S(1)}, bf16[2048,1024]{1,0:T(8,128)(2,1)}, u32[]{:S(2)}) copy-start(bf16[2048,1024]{1,0:T(8,128)(2,1)} %get-tuple-element.10) | copy-start | bytes 12582916
  96.0 3.8 %copy-start.3 = (f32[2,16,1024]{2,1,0:T(8,128)S(1)}, f32[2,16,1024]{2,1,0:T(8,128)}, u32[]{:S(2)}) copy-start(f32[2,16,1024]{2,1,0:T(8,128)} %param.10) | copy-start | bytes 393220
  121.4 2.4 %copy-start.1 = (bf16[2048,1024]{1,0:T(8,128)(2,1)S(1)}, bf16[2048,1024]{1,0:T(8,128)(2,1)}, u32[]{:S(2)}) copy-start(bf16[2048,1024]{1,0:T(8,128)(2,1)} %get-tuple-element.10) | copy-start | bytes 12582916
  121.4 2.4 %copy-start.2 = (bf16[8,32,128]{2,1,0:T(8,128)(2,1)S(1)}, bf16[8,32,128]{2,1,0:T(8,128)(2,1)}, u32[]{:S(2)}) copy-start(bf16[8,32,128]{2,1,0:T(8,128)(2,1)} %far_misfit.1) | copy-start | bytes 196612

commit v3 on v2

--- a/solution.py
+++ b/solution.py
@@ -76,29 +76,33 @@
     return pad_rows(left), pad_rows(right)
 
 
-def horner(coefs, z, scale):
-    total = coefs[-1] * scale
-    for c in coefs[-2::-1]:
-        total = total * z + c * scale
+def monic(coefs, z):
+    total = z + coefs[-2] / coefs[-1]
+    for c in coefs[-3::-1]:
+        total = total * z + c / coefs[-1]
     return total
+
+
+def fraction(t):
+    return t - ((t + MAGIC) - MAGIC)
 
 
 def green(d2):
     inv = lax.rsqrt(d2)
-    t = d2 * inv
-    r = t - ((t + MAGIC) - MAGIC)
+    r = fraction(d2 * inv)
     z = r * r
-    cos_k = horner(COS, z, TURNS) * inv
-    sin_k = horner(SIN, z, TURNS) * (r * inv)
+    cos_k = monic(COS, z) * inv
+    sin_k = monic(SIN, z) * (r * inv)
     return cos_k.astype(bf16), sin_k.astype(bf16)
+
+
+def strips(rows):
+    step = min(rows, 32)
+    return [slice(i, i + step) for i in range(0, rows, step)]
 
 
 def mm(a, b):
     return lax.dot_general(a, b, (((1,), (0,)), ((), ())), preferred_element_type=f32)
-
-
-def mt(a, b):
-    return lax.dot_general(a, b, (((1,), (1,)), ((), ())), preferred_element_type=f32)
 
 
 def chunk_of(total, most):
@@ -148,37 +152,13 @@
 DMA = pltpu.SemaphoreType.DMA
 
 
-def gather_body(name, x_ref, o_ref, send, recv):
-    me = lax.axis_index(name)
-    o_ref[me] = x_ref[...]
-    meet(name)
-    for peer in peers_of(name):
-        push(x_ref, o_ref.at[me], send.at[peer], recv.at[me], name, peer).start()
-    for peer in peers_of(name):
-        done = push(x_ref, o_ref.at[peer], send.at[peer], recv.at[peer], name, peer)
-        done.wait_send()
-        done.wait_recv()
-
-
-def gather(x, name, size, collective_id):
-    return pl.pallas_call(
-        lambda *refs: gather_body(name, *refs),
-        in_specs=[VM],
-        out_specs=VM,
-        out_shape=jax.ShapeDtypeStruct((size, *x.shape), x.dtype),
-        scratch_shapes=[DMA((size,)), DMA((size,))],
-        compiler_params=params(collective_id),
-        name="gather_" + name,
-    )(x)
-
-
 def forward_body(
     a_ref, b_ref, v_ref,
     c_out, s_out, vg_ref, image_ref,
-    c_ref, s_ref, part_ref, vb_ref, u_ref, ur_ref,
-    send_a, recv_a, send_b, recv_b, send_u, recv_u, sem_c, sem_s,
+    c_ref, s_ref, geo_ref, at_ref, part_ref, vb_ref, u_ref, ur_ref,
+    send_x, recv_x, send_a, recv_a, send_b, recv_b, send_u, recv_u, sem_c, sem_s,
 ):
-    blocks, sub = a_ref.shape[:2]
+    blocks, sub = at_ref.shape[:2]
     nb, _, tb = b_ref.shape
     groups, pair = v_ref.shape[:2]
     half = pair // 2
@@ -188,14 +168,17 @@
     spot = lax.axis_index("elem")
 
     def make(j, e):
-        cos_k, sin_k = green(mm(a_ref[e], b_ref[j]))
-        c_ref[j, e] = cos_k
-        s_ref[j, e] = sin_k
+        d2 = mm(at_ref[e], b_ref[j])
+        for strip in strips(sub):
+            cos_k, sin_k = green(d2[strip])
+            c_ref[j, e, strip, :] = cos_k
+            s_ref[j, e, strip, :] = sin_k
 
     def use(j, e):
         va = vg_ref[e].reshape(lanes, sub)
         vb = vb_ref[e].reshape(lanes, sub)
-        u_ref[j] += (mm(va, c_ref[j, e]) + mm(vb, s_ref[j, e])).reshape(groups, pair, tb)
+        total = (TURNS * COS[-1]) * mm(va, c_ref[j, e]) + (TURNS * SIN[-1]) * mm(vb, s_ref[j, e])
+        u_ref[j] += total.reshape(groups, pair, tb)
 
     def start_out(j):
         pltpu.make_async_copy(c_ref.at[j], c_out.at[j], sem_c.at[j]).start()
@@ -230,12 +213,23 @@
         return carry
 
     part_ref[me] = v_ref[me]
+    geo_ref[spot] = a_ref[...]
     meet("dir", "elem")
+    for peer in peers_of("elem"):
+        push(
+            a_ref, geo_ref.at[spot], send_x.at[peer], recv_x.at[spot], "elem", peer
+        ).start()
     for peer in peers_of("dir"):
         push(
             v_ref.at[peer], part_ref.at[me], send_a.at[peer], recv_a.at[me], "dir", peer
         ).start()
     u_ref[...] = jnp.zeros_like(u_ref)
+    for peer in peers_of("elem"):
+        done = push(a_ref, geo_ref.at[peer], send_x.at[peer], recv_x.at[peer], "elem", peer)
+        done.wait_send()
+        done.wait_recv()
+    for e in range(blocks):
+        at_ref[e] = geo_ref[e].astype(f32).T.astype(bf16)
     make_only(0, 0)
     for peer in peers_of("dir"):
         done = push(
@@ -277,8 +271,8 @@
         pltpu.make_async_copy(s_ref.at[j], s_out.at[j], sem_s.at[j]).wait()
 
 
-def forward(a, b, v):
-    blocks, sub = a.shape[:2]
+def forward(a, b, v, blocks):
+    sub = a.shape[1]
     nb, _, tb = b.shape
     groups, pair = v.shape[:2]
     table = (nb, blocks, sub, tb)
@@ -296,10 +290,14 @@
         scratch_shapes=[
             pltpu.VMEM(table, bf16),
             pltpu.VMEM(table, bf16),
+            pltpu.VMEM((blocks, *a.shape), bf16),
+            pltpu.VMEM((blocks, sub, a.shape[0]), bf16),
             pltpu.VMEM((groups, pair, sub), bf16),
             pltpu.VMEM((blocks, groups, pair, sub), bf16),
             pltpu.VMEM((nb, groups, pair, tb), f32),
             pltpu.VMEM((groups, nb, pair, tb), f32),
+            DMA((blocks,)),
+            DMA((blocks,)),
             DMA((groups,)),
             DMA((groups,)),
             DMA((blocks,)),
@@ -320,7 +318,7 @@
 def backward_body(
     mu_ref, c_ref, s_ref, v_ref,
     o_ref,
-    ma_ref, mb_ref, g_ref, gr_ref, all_ref,
+    ma_ref, mat_ref, mbt_ref, g_ref, gr_ref, all_ref,
     send_m, recv_m, send_g, recv_g, send_o, recv_o,
 ):
     e = pl.program_id(0)
@@ -344,14 +342,19 @@
             )
             done.wait_send()
             done.wait_recv()
-        mb_ref[:, :half] = ma_ref[:, half:]
-        mb_ref[:, half:] = -ma_ref[:, :half]
-
-    nu = jnp.zeros((lanes, sub), f32)
-    for j in range(nb):
-        cols = slice(j * tb, (j + 1) * tb)
-        nu += mt(ma_ref[:, :, cols].reshape(lanes, tb), c_ref[j, 0])
-        nu += mt(mb_ref[:, :, cols].reshape(lanes, tb), s_ref[j, 0])
+        for j in range(nb):
+            cols = slice(j * tb, (j + 1) * tb)
+            ma = ma_ref[:, :, cols].astype(f32)
+            mb = jnp.concatenate([ma[:, half:], -ma[:, :half]], axis=1)
+            mat_ref[j] = ma.reshape(lanes, tb).T.astype(bf16)
+            mbt_ref[j] = mb.reshape(lanes, tb).T.astype(bf16)
+
+    first = mm(c_ref[0, 0], mat_ref[0])
+    second = mm(s_ref[0, 0], mbt_ref[0])
+    for j in range(1, nb):
+        first += mm(c_ref[j, 0], mat_ref[j])
+        second += mm(s_ref[j, 0], mbt_ref[j])
+    nu = ((TURNS * COS[-1]) * first + (TURNS * SIN[-1]) * second).T
     v = v_ref[0].reshape(lanes, sub).astype(f32)
     g_ref[e] = jnp.broadcast_to(jnp.sum(nu * v, axis=0, keepdims=True), (8, sub))
 
@@ -395,7 +398,8 @@
         out_shape=jax.ShapeDtypeStruct((groups, 8, sub), f32),
         scratch_shapes=[
             pltpu.VMEM((groups, *mu.shape), bf16),
-            pltpu.VMEM((groups, *mu.shape), bf16),
+            pltpu.VMEM((nb, tb, groups * pair), bf16),
+            pltpu.VMEM((nb, tb, groups * pair), bf16),
             pltpu.VMEM((blocks, 8, sub), f32),
             pltpu.VMEM((blocks, 8, sub), f32),
             pltpu.VMEM((groups, 8, sub), f32),
@@ -458,10 +462,12 @@
     def body(k, carry):
         rows = pl.ds(pl.multiple_of(k * rb, rb), rb)
         t = mm(a_ref[rows, :], b_ref[...])
-        r = t - ((t + MAGIC) - MAGIC)
-        z = r * r
-        c_ref[rows, :] = horner(COS, z, 1.0).astype(bf16)
-        s_ref[rows, :] = (horner(SIN, z, 1.0) * r).astype(bf16)
+        for strip in strips(rb):
+            r = fraction(t[strip])
+            z = r * r
+            part = pl.ds(pl.multiple_of(k * rb + strip.start, strip.stop - strip.start), strip.stop - strip.start)
+            c_ref[part, :] = monic(COS, z).astype(bf16)
+            s_ref[part, :] = (monic(SIN, z) * r).astype(bf16)
         return carry
 
     lax.fori_loop(0, a_ref.shape[0] // rb, body, 0)
@@ -491,8 +497,8 @@
     half = vec.shape[1]
     stacked = vec.reshape(2 * half, vec.shape[2])
     dims = (((1,), (axis,)), ((), ()))
-    first = lax.dot_general(stacked, cos_t, dims, preferred_element_type=f32)
-    second = lax.dot_general(stacked, sin_t, dims, preferred_element_type=f32)
+    first = COS[-1] * lax.dot_general(stacked, cos_t, dims, preferred_element_type=f32)
+    second = SIN[-1] * lax.dot_general(stacked, sin_t, dims, preferred_element_type=f32)
     real = first[:half] - sign * second[half:]
     imag = first[half:] + sign * second[:half]
     return jnp.stack([real, imag])
@@ -513,16 +519,13 @@
     turn_loc = pos_loc * TURNS
 
     src = lax.dynamic_slice_in_dim(turn_loc, me * sub, sub, 1)
-    src = gather(jnp.pad(src, ((0, 5), (0, 0))), "elem", blocks, 0)
-    src = jnp.transpose(src[:, :3], (1, 0, 2)).reshape(3, blocks * sub)
     v = (wz_loc * warm_density).astype(bf16)
     v = jnp.transpose(v.reshape(2 * count_dir, groups, sub), (1, 0, 2))
 
     left, right = distance_rows(src, turn_loc)
     tb = chunk_of(rows, 256)
-    left = left.T.reshape(blocks, sub, left.shape[0])
     right = jnp.transpose(right.reshape(right.shape[0], rows // tb, tb), (1, 0, 2))
-    cos_k, sin_k, v_all, image = forward(left, right, v)
+    cos_k, sin_k, v_all, image = forward(left, right, v, blocks)
     image = image.reshape(2, count_dir, rows)
 
     dvec = lattice(me * count_dir + jnp.arange(count_dir, dtype=jnp.int32), ndir)

time: 159 us -> 158 us (level)
  local copies, waits for them, and re-layouts: 9.11 us -> 7.34 us
    pallas_call x1, Pallas kernels: 59.2 us -> 70.7 us  [forward(): pl.pallas_call(forward_body, in_specs=[VM, VM, VM], out_specs=[HBM, HBM,...]
    pallas_call x1 -> x0, Pallas kernels: 10.7 us -> none  [gather(): pl.pallas_call(lambda *refs: gather_body(name, *refs), in_specs=[VM], out...]
where the time goes in v3:
time: 158 us
  Pallas kernels  136 us (86%)
  other arithmetic  7.84 us (5%)
  local copies, waits for them, and re-layouts  7.34 us (5%)
  matrix products  5.33 us (3%)
    pallas_call x1, Pallas kernels, forward(): pl.pallas_call(forward_body, in_specs=[VM, VM, VM], out_specs=[HBM, HBM,...  70.7 us
    pallas_call x1, Pallas kernels, backward(): pl.pallas_call(backward_body, grid=(blocks,), in_specs=[VM, table, table,...  31.5 us
    pallas_call x1, Pallas kernels, far_misfit(): pl.pallas_call(misfit_body, in_specs=[VM, VM], out_specs=VM, out_shape=ja...  21.8 us
    pallas_call x1, Pallas kernels, far_table(): pl.pallas_call(lambda *refs: table_body(rb, *refs), grid=(recv // tb,), i...  12.2 us
    dot_general x2, matrix products, apply(): lax.dot_general(stacked, cos_t, dims, preferred_element_type=f32)  3.16 us

profile of v3, /device:TPU:0, one launch (start us, length us, event | category | flops | bytes accessed | tf_op | source)
XLA Modules:
  0.0 157.6 jit_solution(10727906962213301468)
XLA Ops:
  0.6 1.3 cosine_multiply_fusion.1
  1.9 0.1 pad_maximum_fusion.3
  2.0 0.3 concatenate.16
  2.3 0.6 pad.20.a_ref
  3.0 0.4 concatenate.17
  3.4 0.7 copy.59
  4.0 0.7 convert_multiply_fusion
  4.8 1.0 multiply_convert_fusion
  5.7 0.1 reshape.150
  5.8 0.7 copy.62
  6.5 0.0 copy-start.4
  6.5 70.7 %forward.1 = (bf16[8,8,512,256]{3,2,1,0:T(8,128)(2,1)}, bf16[8,8,512,256]{3,2,1,0:T(8,128)(2,1)}, bf16[8,4,32,512]{3,2,1,0:T(8,128)(2,1)}, f32[32,2048]{1,0:T(8,128)}) custom-call(bf16[32,512]{1,0:T(8,128)(2,1)} %pad.20.a_ref, bf16[8,32,256]{2,1,0:T(8,128)(2,1)} %bitcast.80, bf16[4,32,512]{2,1,0:T(8,128)(2,1)} %bitcast.81), custom_call_target="tpu_custom_call" | custom-call | flops 4294967296 | bytes 33554432 | tf_op jit(solution)/shard_map/forward/pallas_call | solution.py:280
  77.3 0.1 multiply_reduce_fusion
  77.4 0.5 cosine_bitcast_fusion
  77.9 1.7 %fusion.19 = (f32[2,16,2048]{2,1,0:T(8,128)}, f32[2,16,2048]{2,1,0:T(8,128)S(1)}) fusion(f32[2,16,2048]{2,1,0:T(8,128)} %bitcast.72, f32[1,16,2048]{2,1,0:T(8,128)S(1)} %get-tuple-element.21, f32[1,16,2048]{2,1,0:T(8,128)S(1)} %get-tuple-element.20), kind=kLoop, calls=%fused_computation.85 | loop fusion | flops 131072 | bytes 1048576 | tf_op jit(solution)/shard_map/sub | solution.py:532
  79.6 1.0 fusion.2
  80.6 0.3 concatenate.18
  80.9 0.3 copy.39
  81.2 0.1 pad_bitcast_fusion.refs_0_
  81.3 0.0 copy-done.4
  81.4 0.3 concatenate.19
  81.7 12.2 %far_table.1 = (bf16[2048,1024]{1,0:T(8,128)(2,1)S(1)}, bf16[2048,1024]{1,0:T(8,128)(2,1)}) custom-call(bf16[2048,32]{1,0:T(8,128)(2,1)S(1)} %pad_bitcast_fusion.refs_0_, bf16[32,1024]{1,0:T(8,128)(2,1)S(1)} %pad.23.refs_1_), custom_call_target="tpu_custom_call" | custom-call | flops 62914560 | bytes 8388608 | tf_op jit(solution)/shard_map/far_table/pallas_call | solution.py:484
  93.9 0.0 copy-start
  93.9 0.0 copy-start.3
  93.9 0.8 convolution_multiply_fusion.3
  94.7 1.4 copy-done
  96.1 0.8 convolution_multiply_fusion.2
  97.0 0.7 copy.61
  97.6 0.0 copy-done.3
  97.7 0.7 copy.60
  98.3 21.8 %far_misfit.1 = bf16[8,32,128]{2,1,0:T(8,128)(2,1)} custom-call(f32[8,32,128]{2,1,0:T(8,128)} %bitcast.74, f32[8,32,128]{2,1,0:T(8,128)} %bitcast.76), custom_call_target="tpu_custom_call" | custom-call | tf_op jit(solution)/shard_map/far_misfit/pallas_call | solution.py:450
  120.2 0.0 copy-start.1
  120.2 0.0 copy-start.2
  120.2 2.3 %convolution_multiply_fusion.1 = f32[32,2048]{1,0:T(8,128)S(1)} fusion(bf16[2048,1024]{1,0:T(8,128)(2,1)S(1)} %get-tuple-element.9, bf16[8,32,128]{2,1,0:T(8,128)(2,1)} %far_misfit.1), kind=kOutput, calls=%fused_computation.1 | convolution fusion | flops 134283264 | bytes 4521984 | tf_op jit(solution)/shard_map/dot_general | solution.py:500
  122.5 0.0 copy-done.1
  122.5 0.0 copy-done.2
  122.5 1.4 convolution_multiply_fusion
  124.0 0.7 fusion.mu_ref
  124.6 31.5 %backward.1 = f32[4,8,512]{2,1,0:T(8,128)} custom-call(bf16[32,2048]{1,0:T(8,128)(2,1)} %fusion.mu_ref, bf16[8,8,512,256]{3,2,1,0:T(8,128)(2,1)} %get-tuple-element.11.c_ref, bf16[8,8,512,256]{3,2,1,0:T(8,128)(2,1)} %get-tuple-element.12.s_ref, bf16[8,4,32,512]{3,2,1,0:T(8,128)(2,1)} %get-tuple-element.13.v_ref), custom_call_target="tpu_custom_call" | custom-call | flops 4294967296 | bytes 33554432 | tf_op jit(solution)/shard_map/backward/pallas_call | solution.py:393
  156.1 0.8 slice.43
  157.0 0.6 multiply_divide_fusion
  (19 shorter events, 0.4 us)
Async XLA Ops:
  6.5 74.8 %copy-start.4 = (s32[1024]{0:T(1024)S(1)}, s32[1024]{0:T(1024)}, u32[]{:S(2)}) copy-start(s32[1024]{0:T(1024)} %param.9) | copy-start | bytes 12292
  93.9 2.2 %copy-start = (bf16[2048,1024]{1,0:T(8,128)(2,1)S(1)}, bf16[2048,1024]{1,0:T(8,128)(2,1)}, u32[]{:S(2)}) copy-start(bf16[2048,1024]{1,0:T(8,128)(2,1)} %get-tuple-element.10) | copy-start | bytes 12582916
  93.9 3.8 %copy-start.3 = (f32[2,16,1024]{2,1,0:T(8,128)S(1)}, f32[2,16,1024]{2,1,0:T(8,128)}, u32[]{:S(2)}) copy-start(f32[2,16,1024]{2,1,0:T(8,128)} %param.10) | copy-start | bytes 393220
  120.2 2.4 %copy-start.1 = (bf16[2048,1024]{1,0:T(8,128)(2,1)S(1)}, bf16[2048,1024]{1,0:T(8,128)(2,1)}, u32[]{:S(2)}) copy-start(bf16[2048,1024]{1,0:T(8,128)(2,1)} %get-tuple-element.10) | copy-start | bytes 12582916
  120.2 2.4 %copy-start.2 = (bf16[8,32,128]{2,1,0:T(8,128)(2,1)S(1)}, bf16[8,32,128]{2,1,0:T(8,128)(2,1)}, u32[]{:S(2)}) copy-start(bf16[8,32,128]{2,1,0:T(8,128)(2,1)} %far_misfit.1) | copy-start | bytes 196612

commit v4 on v3

--- a/solution.py
+++ b/solution.py
@@ -103,6 +103,10 @@
 
 def mm(a, b):
     return lax.dot_general(a, b, (((1,), (0,)), ((), ())), preferred_element_type=f32)
+
+
+def mt(a, b):
+    return lax.dot_general(a, b, (((1,), (1,)), ((), ())), preferred_element_type=f32)
 
 
 def chunk_of(total, most):
@@ -191,18 +195,26 @@
                 send_u.at[peer, j], recv_u.at[me, j], "dir", peer,
             ).start()
 
+    def others(act):
+        at = lambda i: lax.rem(spot + i, blocks)
+
+        def two(i, c):
+            act([at(2 * i + 1), at(2 * i + 2)])
+            return c
+
+        pairs = (blocks - 1) // 2
+        lax.fori_loop(0, pairs, two, 0)
+        if blocks - 1 > 2 * pairs:
+            act([at(blocks - 1)])
+
     def make_only(j, carry):
-        lax.fori_loop(0, blocks, lambda e, c: (make(j, e), c)[1], 0)
+        others(lambda es: [make(j, e) for e in es])
         start_out(j)
         return carry
 
     def both(j, carry):
-        def inner(e, c):
-            use(j - lag, e)
-            make(j, e)
-            return c
-
-        lax.fori_loop(0, blocks, inner, 0)
+        others(lambda es: [use(j - lag, e) for e in es] + [make(j, e) for e in es])
+        use(j - lag, spot)
         start_out(j)
         send_block(j - lag)
         return carry
@@ -224,6 +236,13 @@
             v_ref.at[peer], part_ref.at[me], send_a.at[peer], recv_a.at[me], "dir", peer
         ).start()
     u_ref[...] = jnp.zeros_like(u_ref)
+    at_ref[spot] = a_ref[...].astype(f32).T.astype(bf16)
+
+    def make_own(j, carry):
+        make(j, spot)
+        return carry
+
+    lax.fori_loop(0, nb, make_own, 0)
     for peer in peers_of("elem"):
         done = push(a_ref, geo_ref.at[peer], send_x.at[peer], recv_x.at[peer], "elem", peer)
         done.wait_send()
@@ -316,10 +335,10 @@
 
 
 def backward_body(
-    mu_ref, c_ref, s_ref, v_ref,
+    x_ref, data_ref, w_ref, cos_ref, sin_ref, c_ref, s_ref, v_ref,
     o_ref,
-    ma_ref, mat_ref, mbt_ref, g_ref, gr_ref, all_ref,
-    send_m, recv_m, send_g, recv_g, send_o, recv_o,
+    far_ref, got_ref, mis_ref, mu_ref, ma_ref, mat_ref, mbt_ref, g_ref, gr_ref, all_ref,
+    send_f, recv_f, send_r, recv_r, send_m, recv_m, send_g, recv_g, send_o, recv_o,
 ):
     e = pl.program_id(0)
     blocks = pl.num_programs(0)
@@ -332,8 +351,51 @@
 
     @pl.when(e == 0)
     def _():
+        meet("dir", "elem")
+        first = COS[-1] * mm(x_ref[...], cos_ref[...])
+        second = SIN[-1] * mm(x_ref[...], sin_ref[...])
+        far = jnp.concatenate(
+            [first[:half] + second[half:], first[half:] - second[:half]], axis=0
+        )
+        wide = far_ref.shape[2]
+        for k in range(far_ref.shape[0]):
+            far_ref[k] = far[:, k * wide : (k + 1) * wide]
+        got_ref[spot] = far_ref[spot]
+        for peer in peers_of("elem"):
+            push(
+                far_ref.at[peer], got_ref.at[spot],
+                send_f.at[peer], recv_f.at[spot], "elem", peer,
+            ).start()
+        for peer in peers_of("elem"):
+            done = push(
+                far_ref.at[peer], got_ref.at[peer],
+                send_f.at[peer], recv_f.at[peer], "elem", peer,
+            )
+            done.wait_send()
+            done.wait_recv()
+        mis_ref[spot] = (jnp.sum(got_ref[...], axis=0) - data_ref[spot]).astype(bf16)
+        for peer in peers_of("elem"):
+            push(
+                mis_ref.at[spot], mis_ref.at[spot],
+                send_r.at[peer], recv_r.at[spot], "elem", peer,
+            ).start()
+        for peer in peers_of("elem"):
+            done = push(
+                mis_ref.at[spot], mis_ref.at[peer],
+                send_r.at[peer], recv_r.at[peer], "elem", peer,
+            )
+            done.wait_send()
+            done.wait_recv()
+        res = jnp.concatenate([mis_ref[k] for k in range(mis_ref.shape[0])], axis=1)
+        for j in range(nb):
+            cols = slice(j * tb, (j + 1) * tb)
+            first = COS[-1] * mt(res, cos_ref[cols, :])
+            second = SIN[-1] * mt(res, sin_ref[cols, :])
+            mu = jnp.concatenate(
+                [first[:half] - second[half:], first[half:] + second[:half]], axis=0
+            )
+            mu_ref[:, cols] = (w_ref[:, cols] * mu).astype(bf16)
         ma_ref[me] = mu_ref[...]
-        meet("dir", "elem")
         for peer in peers_of("dir"):
             push(mu_ref, ma_ref.at[me], send_m.at[peer], recv_m.at[me], "dir", peer).start()
         for peer in peers_of("dir"):
@@ -385,7 +447,7 @@
         o_ref[...] = all_ref[...]
 
 
-def backward(mu, cos_k, sin_k, v):
+def backward(x, data, w, cos_t, sin_t, cos_k, sin_k, v):
     nb, blocks, sub, tb = cos_k.shape
     groups, pair = v.shape[1:3]
     table = pl.BlockSpec((nb, 1, sub, tb), lambda e: (0, e, 0, 0))
@@ -393,16 +455,24 @@
     return pl.pallas_call(
         backward_body,
         grid=(blocks,),
-        in_specs=[VM, table, table, pl.BlockSpec((1, *v.shape[1:]), lambda e: (e, 0, 0, 0))],
+        in_specs=[VM, VM, VM, VM, VM, table, table, pl.BlockSpec((1, *v.shape[1:]), lambda e: (e, 0, 0, 0))],
         out_specs=VM,
         out_shape=jax.ShapeDtypeStruct((groups, 8, sub), f32),
         scratch_shapes=[
-            pltpu.VMEM((groups, *mu.shape), bf16),
+            pltpu.VMEM(data.shape, f32),
+            pltpu.VMEM(data.shape, f32),
+            pltpu.VMEM(data.shape, bf16),
+            pltpu.VMEM(x.shape, bf16),
+            pltpu.VMEM((groups, *x.shape), bf16),
             pltpu.VMEM((nb, tb, groups * pair), bf16),
             pltpu.VMEM((nb, tb, groups * pair), bf16),
             pltpu.VMEM((blocks, 8, sub), f32),
             pltpu.VMEM((blocks, 8, sub), f32),
             pltpu.VMEM((groups, 8, sub), f32),
+            DMA((blocks,)),
+            DMA((blocks,)),
+            DMA((blocks,)),
+            DMA((blocks,)),
             DMA((groups,)),
             DMA((groups,)),
             DMA((blocks,)),
@@ -415,47 +485,7 @@
             flops=cells * 4 * groups * pair, bytes_accessed=4 * cells, transcendentals=0
         ),
         name="backward",
-    )(mu, cos_k, sin_k, v)
-
-
-def misfit_body(x_ref, data_ref, o_ref, got_ref, send_x, recv_x, send_o, recv_o):
-    me = lax.axis_index("elem")
-    got_ref[me] = x_ref[me]
-    meet("elem")
-    for peer in peers_of("elem"):
-        push(
-            x_ref.at[peer], got_ref.at[me], send_x.at[peer], recv_x.at[me], "elem", peer
-        ).start()
-    for peer in peers_of("elem"):
-        done = push(
-            x_ref.at[peer], got_ref.at[peer], send_x.at[peer], recv_x.at[peer], "elem", peer
-        )
-        done.wait_send()
-        done.wait_recv()
-    o_ref[me] = (jnp.sum(got_ref[...], axis=0) - data_ref[me]).astype(bf16)
-    for peer in peers_of("elem"):
-        push(
-            o_ref.at[me], o_ref.at[me], send_o.at[peer], recv_o.at[me], "elem", peer
-        ).start()
-    for peer in peers_of("elem"):
-        done = push(
-            o_ref.at[me], o_ref.at[peer], send_o.at[peer], recv_o.at[peer], "elem", peer
-        )
-        done.wait_send()
-        done.wait_recv()
-
-
-def far_misfit(x, data):
-    blocks = x.shape[0]
-    return pl.pallas_call(
-        misfit_body,
-        in_specs=[VM, VM],
-        out_specs=VM,
-        out_shape=jax.ShapeDtypeStruct(x.shape, bf16),
-        scratch_shapes=[pltpu.VMEM(x.shape, f32)] + [DMA((blocks,))] * 4,
-        compiler_params=params(3),
-        name="far_misfit",
-    )(x, data)
+    )(x, data, w, cos_t, sin_t, cos_k, sin_k, v)
 
 
 def table_body(rb, a_ref, b_ref, c_ref, s_ref):
@@ -477,7 +507,7 @@
     rows = a.shape[0]
     recv = b.shape[1]
     tb = chunk_of(recv, 256)
-    rb = chunk_of(rows, 256)
+    rb = chunk_of(rows, 512)
     col = lambda n: pl.BlockSpec((n, tb), lambda i: (0, i))
     out = jax.ShapeDtypeStruct((rows, recv), bf16)
     cells = rows * recv
@@ -493,17 +523,6 @@
     )(a, b)
 
 
-def apply(vec, cos_t, sin_t, sign, axis):
-    half = vec.shape[1]
-    stacked = vec.reshape(2 * half, vec.shape[2])
-    dims = (((1,), (axis,)), ((), ()))
-    first = COS[-1] * lax.dot_general(stacked, cos_t, dims, preferred_element_type=f32)
-    second = SIN[-1] * lax.dot_general(stacked, sin_t, dims, preferred_element_type=f32)
-    real = first[:half] - sign * second[half:]
-    imag = first[half:] + sign * second[:half]
-    return jnp.stack([real, imag])
-
-
 def on_device(panel_angles, impedance, quad_count, receivers, farfield_data, warm_density):
     rows = impedance.shape[0]
     count_dir = farfield_data.shape[1]
@@ -533,18 +552,11 @@
 
     left, right = product_rows(turn_loc, lattice(receivers, RBANK))
     cos_t, sin_t = far_table(pad_rows(left).T, pad_rows(right))
-    partial_far = apply((w_loc * state).astype(bf16), cos_t, sin_t, -1.0, 0)
     pair = 2 * count_dir
     recv = farfield_data.shape[2]
-
-    def split(x):
-        return jnp.transpose(x.reshape(pair, blocks, recv // blocks), (1, 0, 2))
-
-    misfit = far_misfit(split(partial_far), split(farfield_data))
-    misfit = jnp.transpose(misfit, (1, 0, 2)).reshape(2, count_dir, recv)
-    adjoint = (w_loc * apply(misfit, cos_t, sin_t, 1.0, 1)).astype(bf16)
-
-    grad = backward(adjoint.reshape(pair, rows), cos_k, sin_k, v_all)
+    data = jnp.transpose(farfield_data.reshape(pair, blocks, recv // blocks), (1, 0, 2))
+    moved = (w_loc * state).astype(bf16).reshape(pair, rows)
+    grad = backward(moved, data, w_loc[None], cos_t, sin_t, cos_k, sin_k, v_all)
     return (grad[:, 0].reshape(rows) / (-ndir * wz_loc), state)
 
 

time: 158 us -> 148 us (0.937)
  matrix products: 5.33 us -> 0 us
  Pallas kernels: 136 us -> 132 us
    dot_general x4 -> x0, matrix products: 5.33 us -> none  [the longest x2 3.16 us: apply(): lax.dot_general(stacked, cos_t, dims, preferred_element_type=f32)]
    pallas_call x1, Pallas kernels: 70.7 us -> 66.4 us  [forward(): pl.pallas_call(forward_body, in_specs=[VM, VM, VM], out_specs=[HBM, HBM,...]
    pallas_call x2 -> x1, Pallas kernels: 53.3 us -> 55.4 us  [backward(): pl.pallas_call(backward_body, grid=(blocks,), in_specs=[VM, VM, VM, VM, V...]
    pallas_call x1, Pallas kernels: 12.2 us -> 10.1 us  [far_table(): pl.pallas_call(lambda *refs: table_body(rb, *refs), grid=(recv // tb,), i...]
where the time goes in v4:
time: 148 us
  Pallas kernels  132 us (89%)
  other arithmetic  7.73 us (5%)
  local copies, waits for them, and re-layouts  7.26 us (5%)
    pallas_call x1, Pallas kernels, forward(): pl.pallas_call(forward_body, in_specs=[VM, VM, VM], out_specs=[HBM, HBM,...  66.4 us
    pallas_call x1, Pallas kernels, backward(): pl.pallas_call(backward_body, grid=(blocks,), in_specs=[VM, VM, VM, VM, V...  55.4 us
    pallas_call x1, Pallas kernels, far_table(): pl.pallas_call(lambda *refs: table_body(rb, *refs), grid=(recv // tb,), i...  10.1 us

profile of v4, /device:TPU:0, one launch (start us, length us, event | category | flops | bytes accessed | tf_op | source)
XLA Modules:
  0.0 147.7 jit_solution(213044698713240443)
XLA Ops:
  0.6 0.0 copy-start.3
  0.6 0.0 copy-start.1
  0.6 1.3 cosine_multiply_fusion.1
  1.9 0.1 pad_maximum_fusion.1
  2.1 0.3 concatenate.16
  2.3 0.6 pad.20.a_ref
  3.0 0.4 concatenate.17
  3.4 0.7 copy.40
  4.1 0.7 convert_multiply_fusion
  4.8 0.0 copy-start.2
  4.8 1.0 multiply_convert_fusion
  5.8 0.1 reshape.145
  5.8 0.7 copy.42
  6.5 66.4 %forward.1 = (bf16[8,8,512,256]{3,2,1,0:T(8,128)(2,1)}, bf16[8,8,512,256]{3,2,1,0:T(8,128)(2,1)}, bf16[8,4,32,512]{3,2,1,0:T(8,128)(2,1)}, f32[32,2048]{1,0:T(8,128)}) custom-call(bf16[32,512]{1,0:T(8,128)(2,1)} %pad.20.a_ref, bf16[8,32,256]{2,1,0:T(8,128)(2,1)} %bitcast.41, bf16[4,32,512]{2,1,0:T(8,128)(2,1)} %bitcast.42), custom_call_target="tpu_custom_call" | custom-call | flops 4294967296 | bytes 33554432 | tf_op jit(solution)/shard_map/forward/pallas_call | solution.py:299
  73.0 0.1 multiply_reduce_fusion
  73.1 0.5 cosine_bitcast_fusion
  73.6 1.7 %fusion.8 = (f32[2,16,2048]{2,1,0:T(8,128)}, f32[2,16,2048]{2,1,0:T(8,128)S(1)}) fusion(f32[2,16,2048]{2,1,0:T(8,128)} %bitcast.36, f32[1,16,2048]{2,1,0:T(8,128)S(1)} %get-tuple-element.17, f32[1,16,2048]{2,1,0:T(8,128)S(1)} %get-tuple-element.16), kind=kLoop, calls=%fused_computation.62 | loop fusion | flops 131072 | bytes 1048576 | tf_op jit(solution)/shard_map/sub | solution.py:551
  75.3 1.6 %fusion.1.x_ref = bf16[32,2048]{1,0:T(8,128)(2,1)} fusion(f32[32,2048]{1,0:T(8,128)} %get-tuple-element.8, f32[2,16,2048]{2,1,0:T(8,128)S(1)} %get-tuple-element.15, f32[2048]{0:T(1024)S(1)} %get-tuple-element.34), kind=kLoop, calls=%fused_computation.5 | loop fusion | flops 196608 | bytes 663552 | tf_op jit(solution)/shard_map/convert_element_type | solution.py:558
  76.9 0.3 concatenate.18
  77.2 0.3 copy.34
  77.5 0.1 pad_bitcast_fusion.refs_0_
  77.7 0.0 copy-done.3
  77.7 0.3 concatenate.19
  78.0 10.1 %far_table.1 = (bf16[2048,1024]{1,0:T(8,128)(2,1)S(1)}, bf16[2048,1024]{1,0:T(8,128)(2,1)}) custom-call(bf16[2048,32]{1,0:T(8,128)(2,1)S(1)} %pad_bitcast_fusion.refs_0_, bf16[32,1024]{1,0:T(8,128)(2,1)S(1)} %pad.23.refs_1_), custom_call_target="tpu_custom_call" | custom-call | flops 62914560 | bytes 8388608 | tf_op jit(solution)/shard_map/far_table/pallas_call | solution.py:514
  88.2 0.0 copy-start
  88.2 2.0 %copy-done = bf16[2048,1024]{1,0:T(8,128)(2,1)} copy-done((bf16[2048,1024]{1,0:T(8,128)(2,1)}, bf16[2048,1024]{1,0:T(8,128)(2,1)S(1)}, u32[]{:S(2)}) %copy-start) | copy-done | bytes 4194328
  90.1 0.0 copy-done.1
  90.2 0.7 copy.41
  90.8 0.0 copy-done.2
  90.9 55.4 %backward.1 = f32[4,8,512]{2,1,0:T(8,128)} custom-call(bf16[32,2048]{1,0:T(8,128)(2,1)} %fusion.1.x_ref, f32[8,32,128]{2,1,0:T(8,128)} %bitcast.37, f32[1,2048]{1,0:T(1,128)} %bitcast.43, bf16[2048,1024]{1,0:T(8,128)(2,1)} %copy-done, bf16[2048,1024]{1,0:T(8,128)(2,1)} %get-tuple-element.10.sin_ref, bf16[8,8,512,256]{3,2,1,0:T(8,128)(2,1)} %get-tuple-element.11.c_ref, ...), custom_call_target="tpu_custom_call" | custom-call | flops 4294967296 | bytes 33554432 | tf_op jit(solution)/shard_map/backward/pallas_call | solution.py:455
  146.2 0.8 slice.11
  147.1 0.6 multiply_divide_fusion
  (14 shorter events, 0.3 us)
Async XLA Ops:
  0.6 77.0 %copy-start.3 = (s32[1024]{0:T(1024)S(1)}, s32[1024]{0:T(1024)}, u32[]{:S(2)}) copy-start(s32[1024]{0:T(1024)} %param.9) | copy-start | bytes 12292
  0.6 89.5 %copy-start.1 = (f32[2,16,1024]{2,1,0:T(8,128)S(1)}, f32[2,16,1024]{2,1,0:T(8,128)}, u32[]{:S(2)}) copy-start(f32[2,16,1024]{2,1,0:T(8,128)} %param.10) | copy-start | bytes 393220
  4.8 86.1 %copy-start.2 = (f32[2048]{0:T(1024)}, f32[2048]{0:T(1024)S(1)}, u32[]{:S(2)}) copy-start(f32[2048]{0:T(1024)S(1)} %get-tuple-element.34) | copy-start | bytes 24580
  88.2 2.0 %copy-start = (bf16[2048,1024]{1,0:T(8,128)(2,1)}, bf16[2048,1024]{1,0:T(8,128)(2,1)S(1)}, u32[]{:S(2)}) copy-start(bf16[2048,1024]{1,0:T(8,128)(2,1)S(1)} %get-tuple-element.9.cos_ref) | copy-start | bytes 12582916

commit v5 on v4

--- a/solution.py
+++ b/solution.py
@@ -15,8 +15,8 @@
 TURNS = WAVENUM / (2.0 * math.pi)
 MAGIC = 12582912.0
 
-COS = (0.99999921, -19.73898036, 64.92865742, -85.27162153, 58.79049212, -21.07110563)
-SIN = (6.28316113, -41.33683183, 81.44770647, -74.9094197, 33.54835515)
+COS = (1.41420401, -6.97763732, 5.71518787, -1.72821389)
+SIN = (4.44287957, -7.30781668, 3.59777418, -0.791199392)
 
 f32 = jnp.float32
 bf16 = jnp.bfloat16
@@ -76,24 +76,24 @@
     return pad_rows(left), pad_rows(right)
 
 
-def monic(coefs, z):
-    total = z + coefs[-2] / coefs[-1]
+def horner(coefs, z):
+    total = coefs[-1] * z + coefs[-2]
     for c in coefs[-3::-1]:
-        total = total * z + c / coefs[-1]
+        total = total * z + c
     return total
 
 
-def fraction(t):
-    return t - ((t + MAGIC) - MAGIC)
+def half_turn(t):
+    r = t - ((t + MAGIC) - MAGIC)
+    z = r * r
+    return horner(COS, z), horner(SIN, z) * r
 
 
 def green(d2):
     inv = lax.rsqrt(d2)
-    r = fraction(d2 * inv)
-    z = r * r
-    cos_k = monic(COS, z) * inv
-    sin_k = monic(SIN, z) * (r * inv)
-    return cos_k.astype(bf16), sin_k.astype(bf16)
+    c, s = half_turn(d2 * inv)
+    over = s * inv
+    return (inv - s * over).astype(bf16), (c * over).astype(bf16)
 
 
 def strips(rows):
@@ -167,7 +167,7 @@
     groups, pair = v_ref.shape[:2]
     half = pair // 2
     lanes = groups * pair
-    lag = nb // 2
+    lag = max(1, (3 * nb) // 8)
     me = lax.axis_index("dir")
     spot = lax.axis_index("elem")
 
@@ -181,7 +181,7 @@
     def use(j, e):
         va = vg_ref[e].reshape(lanes, sub)
         vb = vb_ref[e].reshape(lanes, sub)
-        total = (TURNS * COS[-1]) * mm(va, c_ref[j, e]) + (TURNS * SIN[-1]) * mm(vb, s_ref[j, e])
+        total = TURNS * (mm(va, c_ref[j, e]) + mm(vb, s_ref[j, e]))
         u_ref[j] += total.reshape(groups, pair, tb)
 
     def start_out(j):
@@ -243,13 +243,6 @@
         return carry
 
     lax.fori_loop(0, nb, make_own, 0)
-    for peer in peers_of("elem"):
-        done = push(a_ref, geo_ref.at[peer], send_x.at[peer], recv_x.at[peer], "elem", peer)
-        done.wait_send()
-        done.wait_recv()
-    for e in range(blocks):
-        at_ref[e] = geo_ref[e].astype(f32).T.astype(bf16)
-    make_only(0, 0)
     for peer in peers_of("dir"):
         done = push(
             v_ref.at[peer], part_ref.at[peer], send_a.at[peer], recv_a.at[peer], "dir", peer
@@ -261,7 +254,13 @@
         push(
             part_ref, vg_ref.at[spot], send_b.at[peer], recv_b.at[spot], "elem", peer
         ).start()
-    lax.fori_loop(1, lag, make_only, 0)
+    for peer in peers_of("elem"):
+        done = push(a_ref, geo_ref.at[peer], send_x.at[peer], recv_x.at[peer], "elem", peer)
+        done.wait_send()
+        done.wait_recv()
+    for e in range(blocks):
+        at_ref[e] = geo_ref[e].astype(f32).T.astype(bf16)
+    lax.fori_loop(0, lag, make_only, 0)
     for peer in peers_of("elem"):
         done = push(
             part_ref, vg_ref.at[peer], send_b.at[peer], recv_b.at[peer], "elem", peer
@@ -352,8 +351,8 @@
     @pl.when(e == 0)
     def _():
         meet("dir", "elem")
-        first = COS[-1] * mm(x_ref[...], cos_ref[...])
-        second = SIN[-1] * mm(x_ref[...], sin_ref[...])
+        first = mm(x_ref[...], cos_ref[...])
+        second = mm(x_ref[...], sin_ref[...])
         far = jnp.concatenate(
             [first[:half] + second[half:], first[half:] - second[:half]], axis=0
         )
@@ -389,8 +388,8 @@
         res = jnp.concatenate([mis_ref[k] for k in range(mis_ref.shape[0])], axis=1)
         for j in range(nb):
             cols = slice(j * tb, (j + 1) * tb)
-            first = COS[-1] * mt(res, cos_ref[cols, :])
-            second = SIN[-1] * mt(res, sin_ref[cols, :])
+            first = mt(res, cos_ref[cols, :])
+            second = mt(res, sin_ref[cols, :])
             mu = jnp.concatenate(
                 [first[:half] - second[half:], first[half:] + second[:half]], axis=0
             )
@@ -416,7 +415,7 @@
     for j in range(1, nb):
         first += mm(c_ref[j, 0], mat_ref[j])
         second += mm(s_ref[j, 0], mbt_ref[j])
-    nu = ((TURNS * COS[-1]) * first + (TURNS * SIN[-1]) * second).T
+    nu = (TURNS * (first + second)).T
     v = v_ref[0].reshape(lanes, sub).astype(f32)
     g_ref[e] = jnp.broadcast_to(jnp.sum(nu * v, axis=0, keepdims=True), (8, sub))
 
@@ -493,11 +492,10 @@
         rows = pl.ds(pl.multiple_of(k * rb, rb), rb)
         t = mm(a_ref[rows, :], b_ref[...])
         for strip in strips(rb):
-            r = fraction(t[strip])
-            z = r * r
+            cos_h, sin_h = half_turn(t[strip])
             part = pl.ds(pl.multiple_of(k * rb + strip.start, strip.stop - strip.start), strip.stop - strip.start)
-            c_ref[part, :] = monic(COS, z).astype(bf16)
-            s_ref[part, :] = (monic(SIN, z) * r).astype(bf16)
+            c_ref[part, :] = (1.0 - sin_h * sin_h).astype(bf16)
+            s_ref[part, :] = (cos_h * sin_h).astype(bf16)
         return carry
 
     lax.fori_loop(0, a_ref.shape[0] // rb, body, 0)
@@ -507,7 +505,7 @@
     rows = a.shape[0]
     recv = b.shape[1]
     tb = chunk_of(recv, 256)
-    rb = chunk_of(rows, 512)
+    rb = chunk_of(rows, 1024)
     col = lambda n: pl.BlockSpec((n, tb), lambda i: (0, i))
     out = jax.ShapeDtypeStruct((rows, recv), bf16)
     cells = rows * recv

time: 148 us -> 142 us (0.959)
  Pallas kernels: 132 us -> 126 us
    pallas_call x1, Pallas kernels: 66.4 us -> 61.8 us  [forward(): pl.pallas_call(forward_body, in_specs=[VM, VM, VM], out_specs=[HBM, HBM,...]
where the time goes in v5:
time: 142 us
  Pallas kernels  126 us (89%)
  other arithmetic  7.73 us (5%)
  local copies, waits for them, and re-layouts  7.26 us (5%)
    pallas_call x1, Pallas kernels, forward(): pl.pallas_call(forward_body, in_specs=[VM, VM, VM], out_specs=[HBM, HBM,...  61.8 us
    pallas_call x1, Pallas kernels, backward(): pl.pallas_call(backward_body, grid=(blocks,), in_specs=[VM, VM, VM, VM, V...  55.6 us
    pallas_call x1, Pallas kernels, far_table(): pl.pallas_call(lambda *refs: table_body(rb, *refs), grid=(recv // tb,), i...  8.89 us

profile of v5, /device:TPU:0, one launch (start us, length us, event | category | flops | bytes accessed | tf_op | source)
XLA Modules:
  0.0 142.1 jit_solution(1240681575866950084)
XLA Ops:
  0.6 0.0 copy-start.3
  0.6 0.0 copy-start.1
  0.6 1.3 cosine_multiply_fusion.1
  1.9 0.1 pad_maximum_fusion.1
  2.1 0.3 concatenate.16
  2.3 0.6 pad.20.a_ref
  3.0 0.4 concatenate.17
  3.4 0.7 copy.40
  4.1 0.7 convert_multiply_fusion
  4.8 0.0 copy-start.2
  4.8 1.0 multiply_convert_fusion
  5.8 0.1 reshape.145
  5.8 0.7 copy.42
  6.5 61.8 %forward.1 = (bf16[8,8,512,256]{3,2,1,0:T(8,128)(2,1)}, bf16[8,8,512,256]{3,2,1,0:T(8,128)(2,1)}, bf16[8,4,32,512]{3,2,1,0:T(8,128)(2,1)}, f32[32,2048]{1,0:T(8,128)}) custom-call(bf16[32,512]{1,0:T(8,128)(2,1)} %pad.20.a_ref, bf16[8,32,256]{2,1,0:T(8,128)(2,1)} %bitcast.41, bf16[4,32,512]{2,1,0:T(8,128)(2,1)} %bitcast.42), custom_call_target="tpu_custom_call" | custom-call | flops 4294967296 | bytes 33554432 | tf_op jit(solution)/shard_map/forward/pallas_call | solution.py:298
  68.4 0.1 multiply_reduce_fusion
  68.5 0.5 cosine_bitcast_fusion
  69.0 1.7 %fusion.8 = (f32[2,16,2048]{2,1,0:T(8,128)}, f32[2,16,2048]{2,1,0:T(8,128)S(1)}) fusion(f32[2,16,2048]{2,1,0:T(8,128)} %bitcast.36, f32[1,16,2048]{2,1,0:T(8,128)S(1)} %get-tuple-element.17, f32[1,16,2048]{2,1,0:T(8,128)S(1)} %get-tuple-element.16), kind=kLoop, calls=%fused_computation.62 | loop fusion | flops 131072 | bytes 1048576 | tf_op jit(solution)/shard_map/sub | solution.py:549
  70.7 1.6 %fusion.1.x_ref = bf16[32,2048]{1,0:T(8,128)(2,1)} fusion(f32[32,2048]{1,0:T(8,128)} %get-tuple-element.8, f32[2,16,2048]{2,1,0:T(8,128)S(1)} %get-tuple-element.15, f32[2048]{0:T(1024)S(1)} %get-tuple-element.34), kind=kLoop, calls=%fused_computation.5 | loop fusion | flops 196608 | bytes 663552 | tf_op jit(solution)/shard_map/convert_element_type | solution.py:556
  72.3 0.3 concatenate.18
  72.6 0.3 copy.34
  72.9 0.1 pad_bitcast_fusion.refs_0_
  73.1 0.0 copy-done.3
  73.1 0.3 concatenate.19
  73.5 8.9 %far_table.1 = (bf16[2048,1024]{1,0:T(8,128)(2,1)S(1)}, bf16[2048,1024]{1,0:T(8,128)(2,1)}) custom-call(bf16[2048,32]{1,0:T(8,128)(2,1)S(1)} %pad_bitcast_fusion.refs_0_, bf16[32,1024]{1,0:T(8,128)(2,1)S(1)} %pad.23.refs_1_), custom_call_target="tpu_custom_call" | custom-call | flops 62914560 | bytes 8388608 | tf_op jit(solution)/shard_map/far_table/pallas_call | solution.py:512
  82.3 0.0 copy-start
  82.3 2.0 %copy-done = bf16[2048,1024]{1,0:T(8,128)(2,1)} copy-done((bf16[2048,1024]{1,0:T(8,128)(2,1)}, bf16[2048,1024]{1,0:T(8,128)(2,1)S(1)}, u32[]{:S(2)}) %copy-start) | copy-done | bytes 4194328
  84.3 0.0 copy-done.1
  84.3 0.7 copy.41
  85.0 0.0 copy-done.2
  85.0 55.6 %backward.1 = f32[4,8,512]{2,1,0:T(8,128)} custom-call(bf16[32,2048]{1,0:T(8,128)(2,1)} %fusion.1.x_ref, f32[8,32,128]{2,1,0:T(8,128)} %bitcast.37, f32[1,2048]{1,0:T(1,128)} %bitcast.43, bf16[2048,1024]{1,0:T(8,128)(2,1)} %copy-done, bf16[2048,1024]{1,0:T(8,128)(2,1)} %get-tuple-element.10.sin_ref, bf16[8,8,512,256]{3,2,1,0:T(8,128)(2,1)} %get-tuple-element.11.c_ref, ...), custom_call_target="tpu_custom_call" | custom-call | flops 4294967296 | bytes 33554432 | tf_op jit(solution)/shard_map/backward/pallas_call | solution.py:454
  140.7 0.8 slice.11
  141.5 0.6 multiply_divide_fusion
  (14 shorter events, 0.3 us)
Async XLA Ops:
  0.6 72.4 %copy-start.3 = (s32[1024]{0:T(1024)S(1)}, s32[1024]{0:T(1024)}, u32[]{:S(2)}) copy-start(s32[1024]{0:T(1024)} %param.9) | copy-start | bytes 12292
  0.6 83.7 %copy-start.1 = (f32[2,16,1024]{2,1,0:T(8,128)S(1)}, f32[2,16,1024]{2,1,0:T(8,128)}, u32[]{:S(2)}) copy-start(f32[2,16,1024]{2,1,0:T(8,128)} %param.10) | copy-start | bytes 393220
  4.8 80.2 %copy-start.2 = (f32[2048]{0:T(1024)}, f32[2048]{0:T(1024)S(1)}, u32[]{:S(2)}) copy-start(f32[2048]{0:T(1024)S(1)} %get-tuple-element.34) | copy-start | bytes 24580
  82.3 2.0 %copy-start = (bf16[2048,1024]{1,0:T(8,128)(2,1)}, bf16[2048,1024]{1,0:T(8,128)(2,1)S(1)}, u32[]{:S(2)}) copy-start(bf16[2048,1024]{1,0:T(8,128)(2,1)S(1)} %get-tuple-element.9.cos_ref) | copy-start | bytes 12582916

commit v6 on v5

--- a/solution.py
+++ b/solution.py
@@ -167,7 +167,7 @@
     groups, pair = v_ref.shape[:2]
     half = pair // 2
     lanes = groups * pair
-    lag = max(1, (3 * nb) // 8)
+    lag = max(1, nb // 4)
     me = lax.axis_index("dir")
     spot = lax.axis_index("elem")
 

time: 142 us -> 145 us (1.021)
  Pallas kernels: 126 us -> 129 us
    pallas_call x1, Pallas kernels: 61.8 us -> 64.3 us  [forward(): pl.pallas_call(forward_body, in_specs=[VM, VM, VM], out_specs=[HBM, HBM,...]
where the time goes in v6:
time: 145 us
  Pallas kernels  129 us (89%)
  other arithmetic  7.73 us (5%)
  local copies, waits for them, and re-layouts  7.26 us (5%)
    pallas_call x1, Pallas kernels, forward(): pl.pallas_call(forward_body, in_specs=[VM, VM, VM], out_specs=[HBM, HBM,...  64.3 us
    pallas_call x1, Pallas kernels, backward(): pl.pallas_call(backward_body, grid=(blocks,), in_specs=[VM, VM, VM, VM, V...  55.7 us
    pallas_call x1, Pallas kernels, far_table(): pl.pallas_call(lambda *refs: table_body(rb, *refs), grid=(recv // tb,), i...  8.88 us

profile of v6, /device:TPU:0, one launch (start us, length us, event | category | flops | bytes accessed | tf_op | source)
XLA Modules:
  0.0 144.6 jit_solution(12278588374989260084)
XLA Ops:
  0.6 0.0 copy-start.3
  0.6 0.0 copy-start.1
  0.6 1.3 cosine_multiply_fusion.1
  1.9 0.1 pad_maximum_fusion.1
  2.1 0.3 concatenate.16
  2.3 0.6 pad.20.a_ref
  3.0 0.4 concatenate.17
  3.4 0.7 copy.40
  4.1 0.7 convert_multiply_fusion
  4.8 0.0 copy-start.2
  4.8 1.0 multiply_convert_fusion
  5.8 0.1 reshape.145
  5.8 0.7 copy.42
  6.5 64.3 %forward.1 = (bf16[8,8,512,256]{3,2,1,0:T(8,128)(2,1)}, bf16[8,8,512,256]{3,2,1,0:T(8,128)(2,1)}, bf16[8,4,32,512]{3,2,1,0:T(8,128)(2,1)}, f32[32,2048]{1,0:T(8,128)}) custom-call(bf16[32,512]{1,0:T(8,128)(2,1)} %pad.20.a_ref, bf16[8,32,256]{2,1,0:T(8,128)(2,1)} %bitcast.41, bf16[4,32,512]{2,1,0:T(8,128)(2,1)} %bitcast.42), custom_call_target="tpu_custom_call" | custom-call | flops 4294967296 | bytes 33554432 | tf_op jit(solution)/shard_map/forward/pallas_call | solution.py:298
  70.9 0.1 multiply_reduce_fusion
  71.0 0.5 cosine_bitcast_fusion
  71.5 1.7 %fusion.8 = (f32[2,16,2048]{2,1,0:T(8,128)}, f32[2,16,2048]{2,1,0:T(8,128)S(1)}) fusion(f32[2,16,2048]{2,1,0:T(8,128)} %bitcast.36, f32[1,16,2048]{2,1,0:T(8,128)S(1)} %get-tuple-element.17, f32[1,16,2048]{2,1,0:T(8,128)S(1)} %get-tuple-element.16), kind=kLoop, calls=%fused_computation.62 | loop fusion | flops 131072 | bytes 1048576 | tf_op jit(solution)/shard_map/sub | solution.py:549
  73.1 1.6 %fusion.1.x_ref = bf16[32,2048]{1,0:T(8,128)(2,1)} fusion(f32[32,2048]{1,0:T(8,128)} %get-tuple-element.8, f32[2,16,2048]{2,1,0:T(8,128)S(1)} %get-tuple-element.15, f32[2048]{0:T(1024)S(1)} %get-tuple-element.34), kind=kLoop, calls=%fused_computation.5 | loop fusion | flops 196608 | bytes 663552 | tf_op jit(solution)/shard_map/convert_element_type | solution.py:556
  74.8 0.3 concatenate.18
  75.1 0.3 copy.34
  75.4 0.1 pad_bitcast_fusion.refs_0_
  75.5 0.0 copy-done.3
  75.6 0.3 concatenate.19
  75.9 8.9 %far_table.1 = (bf16[2048,1024]{1,0:T(8,128)(2,1)S(1)}, bf16[2048,1024]{1,0:T(8,128)(2,1)}) custom-call(bf16[2048,32]{1,0:T(8,128)(2,1)S(1)} %pad_bitcast_fusion.refs_0_, bf16[32,1024]{1,0:T(8,128)(2,1)S(1)} %pad.23.refs_1_), custom_call_target="tpu_custom_call" | custom-call | flops 62914560 | bytes 8388608 | tf_op jit(solution)/shard_map/far_table/pallas_call | solution.py:512
  84.8 0.0 copy-start
  84.8 2.0 %copy-done = bf16[2048,1024]{1,0:T(8,128)(2,1)} copy-done((bf16[2048,1024]{1,0:T(8,128)(2,1)}, bf16[2048,1024]{1,0:T(8,128)(2,1)S(1)}, u32[]{:S(2)}) %copy-start) | copy-done | bytes 4194328
  86.8 0.0 copy-done.1
  86.8 0.7 copy.41
  87.5 0.0 copy-done.2
  87.5 55.7 %backward.1 = f32[4,8,512]{2,1,0:T(8,128)} custom-call(bf16[32,2048]{1,0:T(8,128)(2,1)} %fusion.1.x_ref, f32[8,32,128]{2,1,0:T(8,128)} %bitcast.37, f32[1,2048]{1,0:T(1,128)} %bitcast.43, bf16[2048,1024]{1,0:T(8,128)(2,1)} %copy-done, bf16[2048,1024]{1,0:T(8,128)(2,1)} %get-tuple-element.10.sin_ref, bf16[8,8,512,256]{3,2,1,0:T(8,128)(2,1)} %get-tuple-element.11.c_ref, ...), custom_call_target="tpu_custom_call" | custom-call | flops 4294967296 | bytes 33554432 | tf_op jit(solution)/shard_map/backward/pallas_call | solution.py:454
  143.2 0.8 slice.11
  144.0 0.6 multiply_divide_fusion
  (14 shorter events, 0.3 us)
Async XLA Ops:
  0.6 74.9 %copy-start.3 = (s32[1024]{0:T(1024)S(1)}, s32[1024]{0:T(1024)}, u32[]{:S(2)}) copy-start(s32[1024]{0:T(1024)} %param.9) | copy-start | bytes 12292
  0.6 86.1 %copy-start.1 = (f32[2,16,1024]{2,1,0:T(8,128)S(1)}, f32[2,16,1024]{2,1,0:T(8,128)}, u32[]{:S(2)}) copy-start(f32[2,16,1024]{2,1,0:T(8,128)} %param.10) | copy-start | bytes 393220
  4.8 82.7 %copy-start.2 = (f32[2048]{0:T(1024)}, f32[2048]{0:T(1024)S(1)}, u32[]{:S(2)}) copy-start(f32[2048]{0:T(1024)S(1)} %get-tuple-element.34) | copy-start | bytes 24580
  84.8 2.0 %copy-start = (bf16[2048,1024]{1,0:T(8,128)(2,1)}, bf16[2048,1024]{1,0:T(8,128)(2,1)S(1)}, u32[]{:S(2)}) copy-start(bf16[2048,1024]{1,0:T(8,128)(2,1)S(1)} %get-tuple-element.9.cos_ref) | copy-start | bytes 12582916
